TPU v7x, 256 devices: a whole 4x4x8 slice. The times are simulated.
256 devices in a mesh: shard: 8 (over x, core), grp: 32 (over z, y).
Axes of the slice: x: 4, y: 4, z: 8, core: 2. Of those that a mesh axis runs over, the one named last changes fastest.
Arguments:
- sketches: float32 [49152, 1024], P(('shard', 'grp')), may hold values from -6 to 6
- labels: int32 [49152, 1], P(('shard', 'grp')), may hold values from 0 to 7; in each aligned block of 192 rows (0 to 191, 192 to 383, ...) at most 48 rows name the same one
- ranks: int32 [49152], P(('shard', 'grp')), may hold values from 0 to 49151, each once
Outputs:
- highest: float32 [49152], P(('shard', 'grp'))
Inputs may be any that keep to these rules, and one draw needn't show every extreme that they name: `labels`: within the 192 sketches of one device no label occurs more than 48 times; some label occurs exactly 48 times. `ranks`: every rank occurs once.
All inputs are finite; a program needn't handle non-finite values.
Results may differ from a plain program's by a relative error of at most 0.0012.
Values may be sent and summed in bfloat16 or wider, within the bound.
No kernel may reach another device: no remote copies, remote signals or barrier semaphores. Data moves between devices by JAX's collectives and lax.ppermute only.
A program may use at most 64 MiB of HBM per device.

v0:
```python
import jax
import jax.numpy as jnp
from jax import lax
from jax.sharding import PartitionSpec as P

CAP = 48


def block_best(query_rows, query_ranks, key_rows, key_ranks):
    scores = jnp.dot(query_rows, key_rows.T, preferred_element_type=jnp.float32)
    allowed = (key_ranks[None, :] >= 0) & (key_ranks[None, :] < query_ranks[:, None])
    return jnp.max(jnp.where(allowed, scores, jnp.float32(-1.0)), axis=1)


def on_device(sketches, labels, ranks):
    shards = lax.axis_size("shard")
    sum_squares = jnp.sum(sketches * sketches, axis=1, keepdims=True)
    unit = (sketches * lax.rsqrt(sum_squares + 1e-06)).astype(jnp.bfloat16)
    label_ids = labels[:, 0]
    matches = (label_ids[:, None] == jnp.arange(shards, dtype=jnp.int32)[None, :]).astype(jnp.int32)
    position = jnp.sum((jnp.cumsum(matches, axis=0) - 1) * matches, axis=1)
    target = label_ids * CAP + position
    outgoing = jnp.zeros((shards * CAP, unit.shape[1]), jnp.bfloat16).at[target].set(unit)
    out_ranks = jnp.full((shards * CAP,), -1, jnp.int32).at[target].set(ranks)
    inbound, in_ranks = (
        lax.all_to_all(
            outgoing.reshape(shards, CAP, -1), "shard", split_axis=0, concat_axis=0, tiled=True
        ),
        lax.all_to_all(
            out_ranks.reshape(shards, CAP), "shard", split_axis=0, concat_axis=0, tiled=True
        ),
    )
    queries = inbound.reshape(shards * CAP, -1)
    query_ranks = in_ranks.reshape(-1)
    slot_count = queries.shape[0]
    initial = jnp.full((slot_count,), -1.0, jnp.float32)
    best_value = jnp.maximum(
        initial,
        block_best(
            queries,
            query_ranks,
            lax.all_gather(queries, "grp", axis=0, tiled=True),
            lax.all_gather(query_ranks, "grp", axis=0, tiled=True),
        ),
    )
    returned = lax.all_to_all(
        best_value.reshape(shards, CAP), "shard", split_axis=0, concat_axis=0, tiled=True
    ).reshape(-1)
    return returned[target]


def solution(mesh):
    return jax.shard_map(
        on_device,
        mesh=mesh,
        in_specs=(P(("shard", "grp"), None), P(("shard", "grp"), None), P(("shard", "grp"))),
        out_specs=P(("shard", "grp")),
        check_vma=False,
    )
```

profile of v0, /device:TPU:1, one launch (start us, length us, event | category | flops | bytes accessed | tf_op | source)
XLA Modules:
  0.0 253.3 jit_solution(12710394022798061539)
XLA Ops:
  6.5 0.7 iota_compare_fusion
  7.2 0.6 reduce-window.6
  7.8 0.2 slice_reduce_fusion
  8.1 0.7 fusion.4
  8.9 0.7 compare_select_fusion
  9.5 1.3 multiply_reduce_fusion
  10.8 2.3 scatter_custom_fusion.1
  13.1 18.6 %all_to_all.20 = bf16[8,48,1024]{2,1,0:T(8,128)(2,1)} all-to-all(bf16[8,48,1024]{2,1,0:T(8,128)(2,1)S(1)} %bitcast.17), channel_id=1, replica_groups=mesh['shard'=8,'grp'=32] {'shard'}, dimensions={0} | all-to-all | bytes 1572864 | tf_op jit(solution)/shard_map/all_to_all | solution.py:26
  31.7 1.4 scatter_custom_fusion
  33.1 0.1 all_to_all.13
  33.2 8.0 %all_to_all.21 = s32[8,1,48]{2,1,0:T(1,128)S(1)} all-to-all(s32[8,1,48]{2,1,0:T(1,128)S(1)} %all_to_all.13), channel_id=1, replica_groups=mesh['shard'=8,'grp'=32] {'shard'}, dimensions={0} | all-to-all | bytes 3072 | tf_op jit(solution)/shard_map/all_to_all | solution.py:29
  41.1 0.5 broadcast.64
  41.7 0.7 reduce.10
  42.3 0.1 reshape.88
  42.5 42.6 %all-gather = s32[32,1,384]{2,1,0:T(1,128)S(1)} all-gather(s32[1,1,384]{2,1,0:T(1,128)S(1)} %reshape.88), channel_id=1, replica_groups=mesh['shard'=8,'grp'=32] {'grp'}, dimensions={0}, use_global_device_ids=true | all-gather | bytes 50688 | tf_op jit(solution)/shard_map/all_gather | solution.py:43
  85.1 131.3 %all-gather.3.cloned.1.call-done = bf16[12288,1024]{1,0:T(8,128)(2,1)} async-done(((bf16[384,1024]{1,0:T(8,128)(2,1)}), bf16[12288,1024]{1,0:T(8,128)(2,1)}) %all-gather.3.cloned.1.call-update) | async-done | bytes 25165840 | tf_op jit(solution)/shard_map/all_gather | solution.py:42
  216.4 16.0 %select_reduce_fusion = f32[384]{0:T(512)S(1)} fusion(bf16[384,1024]{1,0:T(8,128)(2,1)} %bitcast.16, bf16[12288,1024]{1,0:T(8,128)(2,1)} %all-gather.3.cloned.1.call-done, s32[12288]{0:T(1024)S(1)} %bitcast.19, s32[384]{0:T(512)S(1)} %reshape.59, pred[12288]{0:T(1024)(128)(4,1)S(1)} %broadcast_compare_fusion), kind=kOutput, calls=%fused_computation.3 | convolution fusion | flops 9682550784 | bytes 26016768 | tf_op jit(solution)/shard_map/dot_general | solution.py:10
  232.4 0.7 max_broadcast_in_dim.15
  233.1 5.3 %all-to-all-start.2 = ((f32[8,1,48]{2,1,0:T(1,128)}), f32[8,1,48]{2,1,0:T(1,128)S(1)}, u32[]{:S(2)}, u32[]{:S(2)}) async-start(f32[8,1,48]{2,1,0:T(1,128)} %max_broadcast_in_dim.15), calls=%async_computation.2 | async-start | bytes 8192 | tf_op jit(solution)/shard_map/all_to_all | solution.py:46
  238.4 4.6 %all-to-all-done.2 = f32[8,1,48]{2,1,0:T(1,128)S(1)} async-done(((f32[8,1,48]{2,1,0:T(1,128)}), f32[8,1,48]{2,1,0:T(1,128)S(1)}, u32[]{:S(2)}, u32[]{:S(2)}) %all-to-all-start.2) | async-done | bytes 1568 | tf_op jit(solution)/shard_map/all_to_all | solution.py:46
  243.0 0.5 broadcast.65
  243.5 0.7 reduce.11
  244.2 0.1 reshape.62
  244.2 2.2 gather_fusion
  (11 shorter events, 0.3 us)
Async XLA Ops:
  6.5 209.9 %all-gather.3.cloned.1.call-start = ((), (), s32[]{:S(2)}) async-start(), calls=%async_computation.3 | async-start | bytes 25952256 | tf_op jit(solution)/shard_map/all_gather | solution.py:42
  233.1 9.9 %all-to-all-start.2 = ((f32[8,1,48]{2,1,0:T(1,128)}), f32[8,1,48]{2,1,0:T(1,128)S(1)}, u32[]{:S(2)}, u32[]{:S(2)}) async-start(f32[8,1,48]{2,1,0:T(1,128)} %max_broadcast_in_dim.15), calls=%async_computation.2 | async-start | bytes 8192 | tf_op jit(solution)/shard_map/all_to_all | solution.py:46
Sparse Core Ops, SparseCore 0:
  31.9 184.4 all-gather.2
where the time goes:
time: 254 us; the launch traced here: 253 us
  waiting for transfers between devices  136 us (54%)
  blocking collectives  69.2 us (27%)
  matrix products  16 us (6%)
  between operations  13.4 us (5%)
  other arithmetic  7.72 us (3%)
  local copies, waits for them, and re-layouts  5.77 us (2%)
  starting transfers between devices  5.3 us (2%)
    all_gather x1, waiting for transfers between devices, on_device(): lax.all_gather(queries, 'grp', axis=0, tiled=True)  131 us
    all_gather x1, blocking collectives, on_device(): lax.all_gather(query_ranks, 'grp', axis=0, tiled=True)  42.6 us
    all_to_all x1, blocking collectives, on_device(): lax.all_to_all(outgoing.reshape(shards, CAP, -1), 'shard', split_axis=0,...  18.6 us
    dot_general x1, matrix products, block_best(): scores = jnp.dot(query_rows, key_rows.T, preferred_element_type=jnp.float32)  16 us
    all_to_all x1, blocking collectives, on_device(): lax.all_to_all(out_ranks.reshape(shards, CAP), 'shard', split_axis=0, con...  7.96 us
    all_to_all x1, starting transfers between devices, on_device(): lax.all_to_all(best_value.reshape(shards, CAP), 'shard', split_axis=0, co...  5.3 us
  transfers between devices with their start and end apart: 2, of which 2 were waited for; matrix products, arithmetic and copies ran while one was open for 1% of the time, Pallas kernels for 0%

commit v1 on v0

v1 whole, which is shorter than its diff:
```python
import jax
import jax.numpy as jnp
import numpy as np
from jax import lax
from jax.experimental import pallas as pl
from jax.experimental.pallas import tpu as pltpu
from jax.sharding import Mesh, PartitionSpec as P

AXES = ("x", "core", "z", "y")
SIZES = (4, 2, 8, 4)
ROWS = 192
KEYS = 16
DIM = 1024
FAR = 4.0e9
VMEM = pl.BlockSpec(memory_space=pltpu.VMEM)
SMEM = pl.BlockSpec(memory_space=pltpu.SMEM)


def permutation(move):
    pairs = []
    for source in np.ndindex(*SIZES):
        target = np.array(move(*source)) % np.array(SIZES)
        pairs.append((int(np.ravel_multi_index(source, SIZES)), int(np.ravel_multi_index(tuple(target), SIZES))))
    return pairs


def send(array, move):
    return lax.ppermute(array, AXES, permutation(move))


def call(body, outs, scratch=(), flops=0, spaces=None, count=0, name=None):
    return pl.pallas_call(
        body,
        out_shape=outs,
        in_specs=spaces or [VMEM] * count,
        out_specs=VMEM if isinstance(outs, jax.ShapeDtypeStruct) else [VMEM] * len(outs),
        scratch_shapes=list(scratch),
        compiler_params=pltpu.CompilerParams(vmem_limit_bytes=20 << 20),
        cost_estimate=pl.CostEstimate(flops=flops, bytes_accessed=1 << 20, transcendentals=0),
        name=name,
    )


def column_to_row(column):
    n = column.shape[0]
    diagonal = lax.broadcasted_iota(jnp.int32, (n, n), 0) == lax.broadcasted_iota(jnp.int32, (n, n), 1)
    return jnp.sum(jnp.where(diagonal, column, 0.0), axis=0, keepdims=True)


def row_to_column(row):
    n = row.shape[1]
    diagonal = lax.broadcasted_iota(jnp.int32, (n, n), 0) == lax.broadcasted_iota(jnp.int32, (n, n), 1)
    return jnp.sum(jnp.where(diagonal, row, 0.0), axis=1, keepdims=True)


def normalise_body(sketches, labels, ranks, out):
    values = sketches[...]
    scale = lax.rsqrt(jnp.sum(values * values, axis=1, keepdims=True) + 1e-06)
    out[0:ROWS, :] = (values * scale).astype(jnp.bfloat16)
    label_row = column_to_row(labels[...].astype(jnp.float32))
    rank_row = ranks[...]
    high = (rank_row // 256).astype(jnp.float32)
    low = (rank_row % 256).astype(jnp.float32)
    index = lax.broadcasted_iota(jnp.int32, (KEYS, ROWS), 0)
    rows = jnp.where(index == 0, label_row, jnp.where(index == 1, high, jnp.where(index == 2, low, 0.0)))
    out[ROWS : ROWS + KEYS, :] = jnp.zeros((KEYS, DIM), jnp.bfloat16)
    out[ROWS : ROWS + KEYS, 0:ROWS] = rows.astype(jnp.bfloat16)


def pair_body(core, own, other, out):
    me = core[0]
    first, second = pl.multiple_of(me * ROWS, ROWS), pl.multiple_of((1 - me) * ROWS, ROWS)
    out[pl.ds(first, ROWS), :] = own[0:ROWS, :]
    out[pl.ds(second, ROWS), :] = other[0:ROWS, :]
    mine, theirs = own[ROWS : ROWS + KEYS, :].astype(jnp.float32), other[ROWS : ROWS + KEYS, :].astype(jnp.float32)
    lead, tail = jnp.where(me == 0, mine, theirs), jnp.where(me == 0, theirs, mine)
    out[2 * ROWS : 2 * ROWS + KEYS, :] = jnp.concatenate([lead[0:8], tail[0:8]], axis=0).astype(jnp.bfloat16)


def pick_body(core, both, out):
    me = core[0]
    out[0:ROWS, :] = both[pl.ds(pl.multiple_of(me * ROWS, ROWS), ROWS), :]
    keys = both[2 * ROWS : 2 * ROWS + KEYS, :].astype(jnp.float32)
    chosen = jnp.where(me == 0, keys[0:8], keys[8:16])
    out[ROWS : ROWS + KEYS, :] = jnp.concatenate([chosen, jnp.zeros_like(chosen)], axis=0).astype(jnp.bfloat16)


def key_of(rows):
    return rows[0:1] * 65536.0 + rows[1:2] * 256.0 + rows[2:3]


def bundle_body(a, b, c, d, out):
    columns = []
    for i, block in enumerate((a, b, c, d)):
        out[i * ROWS : (i + 1) * ROWS, :] = block[0:ROWS, :]
        keys = block[ROWS : ROWS + KEYS, 0:256].astype(jnp.float32)[0:8]
        columns.append(jnp.transpose(keys)[0:ROWS])
    rows = jnp.transpose(jnp.concatenate(columns, axis=0))
    out[4 * ROWS : 4 * ROWS + KEYS, :] = jnp.zeros((KEYS, DIM), jnp.bfloat16)
    out[4 * ROWS : 4 * ROWS + KEYS, 0 : 4 * ROWS] = jnp.concatenate([rows, jnp.zeros_like(rows)], axis=0).astype(jnp.bfloat16)


def score(queries, bundles, name):
    refs, layout = [], []
    for bundle in bundles:
        layout.append(len(bundle))
        refs += bundle
    blocks = [q.shape[0] // ROWS for q in queries]
    total = sum(blocks)

    def body(*args):
        q_refs, k_refs, out = args[: len(queries)], list(args[len(queries) : -1]), args[-1]
        parts = []
        for n in layout:
            if n == 1:
                (whole,) = k_refs[:1]
                key_rows = whole[4 * ROWS : 4 * ROWS + KEYS, 0 : 4 * ROWS]
                pieces = [(whole, 256 * j, 256) for j in range(3)]
            else:
                top, bottom = k_refs[:2]
                key_rows = bottom[2 * ROWS : 2 * ROWS + KEYS, 0 : 4 * ROWS]
                pieces = [(top, 0, 384), (bottom, 0, 384)]
            k_refs = k_refs[n:]
            key = key_of(key_rows.astype(jnp.float32)[0:8])
            offset = 0
            for ref, start, length in pieces:
                parts.append((ref, start, length, key[:, offset : offset + length]))
                offset += length
        row = 0
        for q_ref, count in zip(q_refs, blocks):
            size = count * ROWS
            keys = q_ref[size : size + KEYS, 0:256].astype(jnp.float32)
            key_q = jnp.concatenate([jnp.transpose(keys[8 * i : 8 * i + 8])[0:ROWS] for i in range(count)], axis=0)
            key_q = key_q[:, 0:1] * 65536.0 + key_q[:, 1:2] * 256.0 + key_q[:, 2:3]
            base = jnp.floor(key_q * (1.0 / 65536.0)) * 65536.0
            best = jnp.full((size, 128), -1.0, jnp.float32)
            for ref, start, length, key_k in parts:
                scores = lax.dot_general(
                    q_ref[0:size, :], ref[start : start + length, :], (((1,), (1,)), ((), ())), preferred_element_type=jnp.float32
                )
                allowed = (key_k < key_q) & (key_k >= base)
                scores = jnp.where(allowed, scores, -1.0)
                for j in range(0, length, 128):
                    best = jnp.maximum(best, scores[:, j : j + 128])
            top = jnp.max(best, axis=1, keepdims=True)
            for i in range(count):
                out[row : row + 1, :] = column_to_row(top[i * ROWS : (i + 1) * ROWS])
                row += 1

    flops = 2 * DIM * ROWS * ROWS * total * 4 * len(bundles)
    return call(body, jax.ShapeDtypeStruct((total, ROWS), jnp.float32), flops=flops, count=len(queries) + len(refs), name=name)(
        *queries, *refs
    )


def on_device(sketches, labels, ranks):
    block_shape = jax.ShapeDtypeStruct((ROWS + KEYS, DIM), jnp.bfloat16)
    pair_shape = jax.ShapeDtypeStruct((2 * ROWS + KEYS, DIM), jnp.bfloat16)
    bundle_shape = jax.ShapeDtypeStruct((4 * ROWS + KEYS, DIM), jnp.bfloat16)
    core = lax.axis_index("core").astype(jnp.int32)
    z = lax.axis_index("z").astype(jnp.int32)
    place = jnp.stack([core, z])
    own = call(normalise_body, block_shape, count=3, name="normalise")(sketches, labels, ranks.reshape(1, ROWS))

    def first(step):
        return lambda x, c, z, y: (x + step * (1 - c), c, z, y + step * c)

    def second(step):
        return lambda x, c, z, y: (x + step * c, c, z, y + step * (1 - c))

    def along_z(x, c, z, y):
        return (x, c, z + 1 - 2 * c, y)

    def across(x, c, z, y):
        return (x, c + 1, z, y)

    partner = send(own, across)
    line = [own, send(own, first(1)), send(own, first(-1)), send(own, first(2))]
    here = call(pair_body, pair_shape, spaces=[SMEM, VMEM, VMEM], name="pair")(place, own, partner)
    near = send(here, along_z)
    near_other = send(near, across)
    bundle = call(bundle_body, bundle_shape, count=4, name="bundle")(*line)
    after, before = send(bundle, second(-1)), send(bundle, second(1))
    middle = send(near, along_z)
    middle_other = send(middle, across)
    opposite = [send(before[0 : 2 * ROWS], second(1)), send(after[2 * ROWS :], second(-1))]
    far = send(middle, along_z)
    far_other = send(far, across)
    last = send(call(pick_body, block_shape, spaces=[SMEM, VMEM], name="pick")(place, far), along_z)
    last_other = send(last, across)

    s0 = score([here], [[bundle]], "s0")
    s1 = score([near, near_other], [[bundle]], "s1")
    s2 = score([middle, middle_other], [[bundle]], "s2")
    s3 = score([here, near, near_other], [[after], [before]], "s3")
    s4 = score([middle, middle_other], [[after], [before]], "s4")
    s5 = score([far, far_other], [[bundle], [after], [before]], "s5")
    s6 = score([here, near, near_other, middle, middle_other, far, far_other], [opposite], "s6")
    s7 = score([last, last_other], [[bundle], [after], [before], opposite], "s7")

    def merge_body(at, s0, s1, s2, s3, s4, s5, s6, s7, out):
        me, level = at[0], at[1]
        six = s6[...]
        group = {
            0: jnp.maximum(jnp.maximum(s0[...], s3[0:2]), six[0:2]),
            1: jnp.maximum(jnp.maximum(s1[...], s3[2:6]), six[2:6]),
            2: jnp.maximum(jnp.maximum(s2[...], s4[...]), six[6:10]),
            3: jnp.maximum(s5[...], six[10:14]),
        }

        def put(level_of, which, row):
            out[pl.ds(which * 8 + lax.rem(level_of + 16, 8), 1), :] = row

        sign = 2 * me - 1
        put(level, 0, group[0][0:1])
        put(level, 1, group[0][1:2])
        for k in (1, 2, 3):
            put(level + sign * k, 0, group[k][0:1])
            put(level + sign * k, 1, group[k][1:2])
            put(level - sign * k, 0, group[k][2:3])
            put(level - sign * k, 1, group[k][3:4])
        put(level + 4, me, s7[0:1])
        put(level + 4, 1 - me, s7[1:2])

    partial = call(
        merge_body, jax.ShapeDtypeStruct((16, ROWS), jnp.float32), spaces=[SMEM] + [VMEM] * 8, name="merge"
    )(place, s0, s1, s2, s3, s4, s5, s6, s7)
    returned = lax.all_to_all(partial, ("core", "z"), split_axis=0, concat_axis=0, tiled=True)
    return jnp.max(returned, axis=0)


def solution(mesh):
    fine = Mesh(mesh.devices.reshape(SIZES), AXES)
    return jax.shard_map(
        on_device,
        mesh=fine,
        in_specs=(P(AXES, None), P(AXES, None), P(AXES)),
        out_specs=P(AXES),
        check_vma=False,
    )
```

time: 254 us -> 98.1 us (0.39)
  waiting for transfers between devices: 136 us -> 22.4 us
  blocking collectives: 69.2 us -> 12.8 us
  Pallas kernels: 0 us -> 28.7 us
  starting transfers between devices: 5.3 us -> 30.4 us
  matrix products: 16 us -> 0 us
  between operations: 13.4 us -> 0.18 us
  other arithmetic: 7.72 us -> 0.67 us
  local copies, waits for them, and re-layouts: 5.77 us -> 2.72 us
    all_gather x1 -> x0, waiting for transfers between devices: 131 us -> none  [on_device(): lax.all_gather(queries, 'grp', axis=0, tiled=True)]
    all_gather x1 -> x0, blocking collectives: 42.6 us -> none  [on_device(): lax.all_gather(query_ranks, 'grp', axis=0, tiled=True)]
    ppermute x0 -> x16, starting transfers between devices: none -> 30.4 us  [send(): return lax.ppermute(array, AXES, permutation(move))]
    pallas_call x0 -> x13, Pallas kernels: none -> 28.7 us  [the longest x8 26.5 us: score(): call(body, jax.ShapeDtypeStruct((total, ROWS), jnp.float32), flops=flops,...]
    ppermute x0 -> x16, waiting for transfers between devices: none -> 22.4 us  [send(): return lax.ppermute(array, AXES, permutation(move))]
    dot_general x1 -> x0, matrix products: 16 us -> none  [block_best(): scores = jnp.dot(query_rows, key_rows.T, preferred_element_type=jnp.float32)]
    all_to_all x2 -> x1, blocking collectives: 26.5 us -> 12.8 us  [on_device(): lax.all_to_all(partial, ('core', 'z'), split_axis=0, concat_axis=0, tiled...]
    all_to_all x1 -> x0, starting transfers between devices: 5.3 us -> none  [on_device(): lax.all_to_all(best_value.reshape(shards, CAP), 'shard', split_axis=0, co...]
  transfers between devices with their start and end apart: 2 -> 16, of which waited for: 2 -> 6; matrix products, arithmetic and copies ran while one was open for 1% -> 0% of each run, Pallas kernels for 0% -> 23%
where the time goes in v1:
time: 98.1 us; the launch traced here: 97.9 us
  starting transfers between devices  30.4 us (31%)
  Pallas kernels  28.7 us (29%)
  waiting for transfers between devices  22.4 us (23%)
  blocking collectives  12.8 us (13%)
  local copies, waits for them, and re-layouts  2.72 us (3%)
    ppermute x16, starting transfers between devices, send(): return lax.ppermute(array, AXES, permutation(move))  30.4 us
    pallas_call x8, Pallas kernels, score(): call(body, jax.ShapeDtypeStruct((total, ROWS), jnp.float32), flops=flops,...  26.5 us
    ppermute x16, waiting for transfers between devices, send(): return lax.ppermute(array, AXES, permutation(move))  22.4 us
    all_to_all x1, blocking collectives, on_device(): lax.all_to_all(partial, ('core', 'z'), split_axis=0, concat_axis=0, tiled...  12.8 us
    unnamed x5, local copies, waits for them, and re-layouts  2.6 us
  transfers between devices with their start and end apart: 16, of which 6 were waited for; matrix products, arithmetic and copies ran while one was open for 0% of the time, Pallas kernels for 23%

profile of v1, /device:TPU:1, one launch (start us, length us, event | category | flops | bytes accessed | tf_op | source)
XLA Modules:
  0.0 97.9 jit_solution(971154476740676530)
XLA Ops:
  2.8 3.3 %collective-permute-start = (bf16[208,1024]{1,0:T(8,128)(2,1)S(1)}, bf16[208,1024]{1,0:T(8,128)(2,1)S(1)}, u32[]{:S(2)}, u32[]{:S(2)}) collective-permute-start(bf16[208,1024]{1,0:T(8,128)(2,1)S(1)} %normalise.1.own.a), channel_id=1, source_target_pairs={{0,32},{1,33},{2,34},{3,35},{4,36},{5,37},{6,38},{7,39},{8,40},{9,... | collective-permute-start | bytes 1277960 | tf_op jit(solution)/shard_map/ppermute | solution.py:28
  6.2 1.3 %collective-permute-done.other = bf16[208,1024]{1,0:T(8,128)(2,1)S(1)} collective-permute-done((bf16[208,1024]{1,0:T(8,128)(2,1)S(1)}, bf16[208,1024]{1,0:T(8,128)(2,1)S(1)}, u32[]{:S(2)}, u32[]{:S(2)}) %collective-permute-start) | collective-permute-done | bytes 426016 | tf_op jit(solution)/shard_map/ppermute | solution.py:28
  8.1 3.9 %collective-permute-start.4 = (bf16[400,1024]{1,0:T(8,128)(2,1)S(1)}, bf16[400,1024]{1,0:T(8,128)(2,1)S(1)}, u32[]{:S(2)}, u32[]{:S(2)}) collective-permute-start(bf16[400,1024]{1,0:T(8,128)(2,1)S(1)} %pair.1.args_0_), channel_id=1, source_target_pairs={{0,4},{1,5},{2,6},{3,7},{4,8},{5,9},{6,10},{7,11},{8,12},{9,13},{1... | collective-permute-start | bytes 2457608 | tf_op jit(solution)/shard_map/ppermute | solution.py:28
  12.0 1.3 %collective-permute-start.1 = (bf16[208,1024]{1,0:T(8,128)(2,1)S(1)}, bf16[208,1024]{1,0:T(8,128)(2,1)S(1)}, u32[]{:S(2)}, u32[]{:S(2)}) collective-permute-start(bf16[208,1024]{1,0:T(8,128)(2,1)S(1)} %normalise.1.own.a), channel_id=1, source_target_pairs={{0,64},{1,65},{2,66},{3,67},{4,68},{5,69},{6,70},{7,71},{8,72},{9,... | collective-permute-start | bytes 1277960 | tf_op jit(solution)/shard_map/ppermute | solution.py:28
  13.3 1.4 %collective-permute-start.2 = (bf16[208,1024]{1,0:T(8,128)(2,1)S(1)}, bf16[208,1024]{1,0:T(8,128)(2,1)S(1)}, u32[]{:S(2)}, u32[]{:S(2)}) collective-permute-start(bf16[208,1024]{1,0:T(8,128)(2,1)S(1)} %normalise.1.own.a), channel_id=1, source_target_pairs={{0,192},{1,193},{2,194},{3,195},{4,196},{5,197},{6,198},{7,199},{8... | collective-permute-start | bytes 1277960 | tf_op jit(solution)/shard_map/ppermute | solution.py:28
  14.8 1.6 %collective-permute-start.3 = (bf16[208,1024]{1,0:T(8,128)(2,1)S(1)}, bf16[208,1024]{1,0:T(8,128)(2,1)S(1)}, u32[]{:S(2)}, u32[]{:S(2)}) collective-permute-start(bf16[208,1024]{1,0:T(8,128)(2,1)S(1)} %normalise.1.own.a), channel_id=1, source_target_pairs={{0,128},{1,129},{2,130},{3,131},{4,132},{5,133},{6,134},{7,135},{8... | collective-permute-start | bytes 1277960 | tf_op jit(solution)/shard_map/ppermute | solution.py:28
  16.4 4.9 %collective-permute-done.4.args_0_.args_1_ = bf16[400,1024]{1,0:T(8,128)(2,1)S(1)} collective-permute-done((bf16[400,1024]{1,0:T(8,128)(2,1)S(1)}, bf16[400,1024]{1,0:T(8,128)(2,1)S(1)}, u32[]{:S(2)}, u32[]{:S(2)}) %collective-permute-start.4) | collective-permute-done | bytes 819232 | tf_op jit(solution)/shard_map/ppermute | solution.py:28
  21.3 3.4 %collective-permute-start.6 = (bf16[400,1024]{1,0:T(8,128)(2,1)S(1)}, bf16[400,1024]{1,0:T(8,128)(2,1)S(1)}, u32[]{:S(2)}, u32[]{:S(2)}) collective-permute-start(bf16[400,1024]{1,0:T(8,128)(2,1)S(1)} %collective-permute-done.4.args_0_.args_1_), channel_id=1, source_target_pairs={{0,4},{1,5},{2,6},{3,7},{4,8},{5,9},{6,10},{7,11},{8,12},{9,13},{1... | collective-permute-start | bytes 2457608 | tf_op jit(solution)/shard_map/ppermute | solution.py:28
  24.7 1.3 %collective-permute-done.3.d = bf16[208,1024]{1,0:T(8,128)(2,1)S(1)} collective-permute-done((bf16[208,1024]{1,0:T(8,128)(2,1)S(1)}, bf16[208,1024]{1,0:T(8,128)(2,1)S(1)}, u32[]{:S(2)}, u32[]{:S(2)}) %collective-permute-start.3) | collective-permute-done | bytes 426016 | tf_op jit(solution)/shard_map/ppermute | solution.py:28
  26.3 2.5 %collective-permute-start.8 = (bf16[784,1024]{1,0:T(8,128)(2,1)S(1)}, bf16[784,1024]{1,0:T(8,128)(2,1)S(1)}, u32[]{:S(2)}, u32[]{:S(2)}) collective-permute-start(bf16[784,1024]{1,0:T(8,128)(2,1)S(1)} %bundle.1.args_1_.args_2_), channel_id=1, source_target_pairs={{0,3},{1,0},{2,1},{3,2},{4,7},{5,4},{6,5},{7,6},{8,11},{9,8},{10,9... | collective-permute-start | bytes 4816904 | tf_op jit(solution)/shard_map/ppermute | solution.py:28
  28.8 5.2 %collective-permute-done.6.args_0_.args_3_ = bf16[400,1024]{1,0:T(8,128)(2,1)S(1)} collective-permute-done((bf16[400,1024]{1,0:T(8,128)(2,1)S(1)}, bf16[400,1024]{1,0:T(8,128)(2,1)S(1)}, u32[]{:S(2)}, u32[]{:S(2)}) %collective-permute-start.6) | collective-permute-done | bytes 819232 | tf_op jit(solution)/shard_map/ppermute | solution.py:28
  34.0 3.4 %collective-permute-start.10 = (bf16[400,1024]{1,0:T(8,128)(2,1)S(1)}, bf16[400,1024]{1,0:T(8,128)(2,1)S(1)}, u32[]{:S(2)}, u32[]{:S(2)}) collective-permute-start(bf16[400,1024]{1,0:T(8,128)(2,1)S(1)} %collective-permute-done.6.args_0_.args_3_), channel_id=1, source_target_pairs={{0,4},{1,5},{2,6},{3,7},{4,8},{5,9},{6,10},{7,11},{8,12},{9,13},{1... | collective-permute-start | bytes 2457608 | tf_op jit(solution)/shard_map/ppermute | solution.py:28
  37.9 8.8 %collective-permute-done.10.args_0_.args_5_.both = bf16[400,1024]{1,0:T(8,128)(2,1)S(1)} collective-permute-done((bf16[400,1024]{1,0:T(8,128)(2,1)S(1)}, bf16[400,1024]{1,0:T(8,128)(2,1)S(1)}, u32[]{:S(2)}, u32[]{:S(2)}) %collective-permute-start.10) | collective-permute-done | bytes 819232 | tf_op jit(solution)/shard_map/ppermute | solution.py:28
  46.7 3.4 %collective-permute-start.11 = (bf16[400,1024]{1,0:T(8,128)(2,1)S(1)}, bf16[400,1024]{1,0:T(8,128)(2,1)S(1)}, u32[]{:S(2)}, u32[]{:S(2)}) collective-permute-start(bf16[400,1024]{1,0:T(8,128)(2,1)S(1)} %collective-permute-done.10.args_0_.args_5_.both), channel_id=1, source_target_pairs={{0,32},{1,33},{2,34},{3,35},{4,36},{5,37},{6,38},{7,39},{8,40},{9,... | collective-permute-start | bytes 2457608 | tf_op jit(solution)/shard_map/ppermute | solution.py:28
  51.1 2.5 %collective-permute-start.13 = (bf16[400,1024]{1,0:T(8,128)(2,1)S(1)}, bf16[400,1024]{1,0:T(8,128)(2,1)S(1)}, u32[]{:S(2)}, u32[]{:S(2)}) collective-permute-start(bf16[400,1024]{1,0:T(8,128)(2,1)S(1)} %slice.9), channel_id=1, source_target_pairs={{0,3},{1,0},{2,1},{3,2},{4,7},{5,4},{6,5},{7,6},{8,11},{9,8},{10,9... | collective-permute-start | bytes 2457608 | tf_op jit(solution)/shard_map/ppermute | solution.py:28
  54.0 4.4 %s3.1 = f32[6,192]{1,0:T(8,128)S(1)} custom-call(bf16[400,1024]{1,0:T(8,128)(2,1)S(1)} %pair.1.args_0_, bf16[400,1024]{1,0:T(8,128)(2,1)S(1)} %collective-permute-done.4.args_0_.args_1_, bf16[400,1024]{1,0:T(8,128)(2,1)S(1)} %collective-permute-done.5.args_1_.args_2_, bf16[784,1024]{1,0:T(8,128)(2,1)S(1)} %collective-permute-done.8.args_3_.args_2_, ...), custom_call_target="tpu_custom_call" | custom-call | flops 3623878656 | bytes 1048576 | tf_op jit(solution)/shard_map/s3/pallas_call | solution.py:151
  59.1 1.7 %s1_.1.s1 = f32[4,192]{1,0:T(4,128)S(1)} custom-call(bf16[400,1024]{1,0:T(8,128)(2,1)S(1)} %collective-permute-done.4.args_0_.args_1_, bf16[400,1024]{1,0:T(8,128)(2,1)S(1)} %collective-permute-done.5.args_1_.args_2_, bf16[784,1024]{1,0:T(8,128)(2,1)S(1)} %bundle.1.args_1_.args_2_), custom_call_target="tpu_custom_call" | custom-call | flops 1207959552 | bytes 1048576 | tf_op jit(solution)/shard_map/s1/pallas_call | solution.py:151
  60.7 1.6 %s2_.1.s2 = f32[4,192]{1,0:T(4,128)S(1)} custom-call(bf16[400,1024]{1,0:T(8,128)(2,1)S(1)} %collective-permute-done.6.args_0_.args_3_, bf16[400,1024]{1,0:T(8,128)(2,1)S(1)} %collective-permute-done.7.args_1_.args_4_, bf16[784,1024]{1,0:T(8,128)(2,1)S(1)} %bundle.1.args_1_.args_2_), custom_call_target="tpu_custom_call" | custom-call | flops 1207959552 | bytes 1048576 | tf_op jit(solution)/shard_map/s2/pallas_call | solution.py:151
  62.4 3.0 %s4_.1.s4 = f32[4,192]{1,0:T(4,128)S(1)} custom-call(bf16[400,1024]{1,0:T(8,128)(2,1)S(1)} %collective-permute-done.6.args_0_.args_3_, bf16[400,1024]{1,0:T(8,128)(2,1)S(1)} %collective-permute-done.7.args_1_.args_4_, bf16[784,1024]{1,0:T(8,128)(2,1)S(1)} %collective-permute-done.8.args_3_.args_2_, bf16[784,1024]{1,0:T(8,128)(2,1)S(1)} %collective-permute-done.9.args_4_.args_3_), custom_call_target="tpu_custom_call" | custom-call | flops 2415919104 | bytes 1048576 | tf_op jit(solution)/shard_map/s4/pallas_call | solution.py:151
  66.3 2.6 %collective-permute-start.15 = (bf16[208,1024]{1,0:T(8,128)(2,1)S(1)}, bf16[208,1024]{1,0:T(8,128)(2,1)S(1)}, u32[]{:S(2)}, u32[]{:S(2)}) collective-permute-start(bf16[208,1024]{1,0:T(8,128)(2,1)S(1)} %collective-permute-done.14.args_0_), channel_id=1, source_target_pairs={{0,32},{1,33},{2,34},{3,35},{4,36},{5,37},{6,38},{7,39},{8,40},{9,... | collective-permute-start | bytes 1277960 | tf_op jit(solution)/shard_map/ppermute | solution.py:28
  68.9 4.3 %s5.1 = f32[4,192]{1,0:T(4,128)S(1)} custom-call(bf16[400,1024]{1,0:T(8,128)(2,1)S(1)} %collective-permute-done.10.args_0_.args_5_.both, bf16[400,1024]{1,0:T(8,128)(2,1)S(1)} %collective-permute-done.11.args_1_.args_6_, bf16[784,1024]{1,0:T(8,128)(2,1)S(1)} %bundle.1.args_1_.args_2_, bf16[784,1024]{1,0:T(8,128)(2,1)S(1)} %collective-permute-done.8.args_3_.args_2_, ...), custom_call_target="tpu_custom_call" | custom-call | flops 3623878656 | bytes 1048576 | tf_op jit(solution)/shard_map/s5/pallas_call | solution.py:151
  73.3 6.1 %s6.1 = f32[14,192]{1,0:T(8,128)S(1)} custom-call(bf16[400,1024]{1,0:T(8,128)(2,1)S(1)} %pair.1.args_0_, bf16[400,1024]{1,0:T(8,128)(2,1)S(1)} %collective-permute-done.4.args_0_.args_1_, bf16[400,1024]{1,0:T(8,128)(2,1)S(1)} %collective-permute-done.5.args_1_.args_2_, bf16[400,1024]{1,0:T(8,128)(2,1)S(1)} %collective-permute-done.6.args_0_.args_3_, ...), custom_call_target="tpu_custom_call" | custom-call | flops 4227858432 | bytes 1048576 | tf_op jit(solution)/shard_map/s6/pallas_call | solution.py:151
  79.4 4.5 %s7.1 = f32[2,192]{1,0:T(2,128)S(1)} custom-call(bf16[208,1024]{1,0:T(8,128)(2,1)S(1)} %collective-permute-done.14.args_0_, bf16[208,1024]{1,0:T(8,128)(2,1)S(1)} %collective-permute-done.15.args_1_, bf16[784,1024]{1,0:T(8,128)(2,1)S(1)} %bundle.1.args_1_.args_2_, bf16[784,1024]{1,0:T(8,128)(2,1)S(1)} %collective-permute-done.8.args_3_.args_2_, ...), custom_call_target="tpu_custom_call" | custom-call | flops 2415919104 | bytes 1048576 | tf_op jit(solution)/shard_map/s7/pallas_call | solution.py:151
  84.5 12.8 %all_to_all.9 = f32[16,1,192]{2,1,0:T(1,128)S(1)} all-to-all(f32[16,1,192]{2,1,0:T(1,128)S(1)} %copy.6), channel_id=1, replica_groups=mesh['x'=4,'core'=2,'z'=8,'y'=4] {'core','z'}, dimensions={0} | all-to-all | bytes 24576 | tf_op jit(solution)/shard_map/all_to_all | solution.py:228
  (32 shorter events, 8.4 us)
Async XLA Ops:
  0.8 1.1 %copy-start = (f32[192,1024]{1,0:T(8,128)S(1)}, f32[192,1024]{1,0:T(8,128)}, u32[]{:S(2)}) copy-start(f32[192,1024]{1,0:T(8,128)} %sketches.1) | copy-start | bytes 2359300
  1.9 0.7 copy-start.1
  2.8 4.7 %collective-permute-start = (bf16[208,1024]{1,0:T(8,128)(2,1)S(1)}, bf16[208,1024]{1,0:T(8,128)(2,1)S(1)}, u32[]{:S(2)}, u32[]{:S(2)}) collective-permute-start(bf16[208,1024]{1,0:T(8,128)(2,1)S(1)} %normalise.1.own.a), channel_id=1, source_target_pairs={{0,32},{1,33},{2,34},{3,35},{4,36},{5,37},{6,38},{7,39},{8,40},{9,... | collective-permute-start | bytes 1277960 | tf_op jit(solution)/shard_map/ppermute | solution.py:28
  8.1 13.2 %collective-permute-start.4 = (bf16[400,1024]{1,0:T(8,128)(2,1)S(1)}, bf16[400,1024]{1,0:T(8,128)(2,1)S(1)}, u32[]{:S(2)}, u32[]{:S(2)}) collective-permute-start(bf16[400,1024]{1,0:T(8,128)(2,1)S(1)} %pair.1.args_0_), channel_id=1, source_target_pairs={{0,4},{1,5},{2,6},{3,7},{4,8},{5,9},{6,10},{7,11},{8,12},{9,13},{1... | collective-permute-start | bytes 2457608 | tf_op jit(solution)/shard_map/ppermute | solution.py:28
  12.0 12.7 %collective-permute-start.1 = (bf16[208,1024]{1,0:T(8,128)(2,1)S(1)}, bf16[208,1024]{1,0:T(8,128)(2,1)S(1)}, u32[]{:S(2)}, u32[]{:S(2)}) collective-permute-start(bf16[208,1024]{1,0:T(8,128)(2,1)S(1)} %normalise.1.own.a), channel_id=1, source_target_pairs={{0,64},{1,65},{2,66},{3,67},{4,68},{5,69},{6,70},{7,71},{8,72},{9,... | collective-permute-start | bytes 1277960 | tf_op jit(solution)/shard_map/ppermute | solution.py:28
  13.3 11.4 %collective-permute-start.2 = (bf16[208,1024]{1,0:T(8,128)(2,1)S(1)}, bf16[208,1024]{1,0:T(8,128)(2,1)S(1)}, u32[]{:S(2)}, u32[]{:S(2)}) collective-permute-start(bf16[208,1024]{1,0:T(8,128)(2,1)S(1)} %normalise.1.own.a), channel_id=1, source_target_pairs={{0,192},{1,193},{2,194},{3,195},{4,196},{5,197},{6,198},{7,199},{8... | collective-permute-start | bytes 1277960 | tf_op jit(solution)/shard_map/ppermute | solution.py:28
  14.8 11.3 %collective-permute-start.3 = (bf16[208,1024]{1,0:T(8,128)(2,1)S(1)}, bf16[208,1024]{1,0:T(8,128)(2,1)S(1)}, u32[]{:S(2)}, u32[]{:S(2)}) collective-permute-start(bf16[208,1024]{1,0:T(8,128)(2,1)S(1)} %normalise.1.own.a), channel_id=1, source_target_pairs={{0,128},{1,129},{2,130},{3,131},{4,132},{5,133},{6,134},{7,135},{8... | collective-permute-start | bytes 1277960 | tf_op jit(solution)/shard_map/ppermute | solution.py:28
  21.3 12.7 %collective-permute-start.6 = (bf16[400,1024]{1,0:T(8,128)(2,1)S(1)}, bf16[400,1024]{1,0:T(8,128)(2,1)S(1)}, u32[]{:S(2)}, u32[]{:S(2)}) collective-permute-start(bf16[400,1024]{1,0:T(8,128)(2,1)S(1)} %collective-permute-done.4.args_0_.args_1_), channel_id=1, source_target_pairs={{0,4},{1,5},{2,6},{3,7},{4,8},{5,9},{6,10},{7,11},{8,12},{9,13},{1... | collective-permute-start | bytes 2457608 | tf_op jit(solution)/shard_map/ppermute | solution.py:28
  26.3 24.8 %collective-permute-start.8 = (bf16[784,1024]{1,0:T(8,128)(2,1)S(1)}, bf16[784,1024]{1,0:T(8,128)(2,1)S(1)}, u32[]{:S(2)}, u32[]{:S(2)}) collective-permute-start(bf16[784,1024]{1,0:T(8,128)(2,1)S(1)} %bundle.1.args_1_.args_2_), channel_id=1, source_target_pairs={{0,3},{1,0},{2,1},{3,2},{4,7},{5,4},{6,5},{7,6},{8,11},{9,8},{10,9... | collective-permute-start | bytes 4816904 | tf_op jit(solution)/shard_map/ppermute | solution.py:28
  28.8 24.9 %collective-permute-start.9 = (bf16[784,1024]{1,0:T(8,128)(2,1)S(1)}, bf16[784,1024]{1,0:T(8,128)(2,1)S(1)}, u32[]{:S(2)}, u32[]{:S(2)}) collective-permute-start(bf16[784,1024]{1,0:T(8,128)(2,1)S(1)} %bundle.1.args_1_.args_2_), channel_id=1, source_target_pairs={{0,1},{1,2},{2,3},{3,0},{4,5},{5,6},{6,7},{7,4},{8,9},{9,10},{10,1... | collective-permute-start | bytes 4816904 | tf_op jit(solution)/shard_map/ppermute | solution.py:28
  34.0 12.7 %collective-permute-start.10 = (bf16[400,1024]{1,0:T(8,128)(2,1)S(1)}, bf16[400,1024]{1,0:T(8,128)(2,1)S(1)}, u32[]{:S(2)}, u32[]{:S(2)}) collective-permute-start(bf16[400,1024]{1,0:T(8,128)(2,1)S(1)} %collective-permute-done.6.args_0_.args_3_), channel_id=1, source_target_pairs={{0,4},{1,5},{2,6},{3,7},{4,8},{5,9},{6,10},{7,11},{8,12},{9,13},{1... | collective-permute-start | bytes 2457608 | tf_op jit(solution)/shard_map/ppermute | solution.py:28
  37.4 16.6 %collective-permute-start.5 = (bf16[400,1024]{1,0:T(8,128)(2,1)S(1)}, bf16[400,1024]{1,0:T(8,128)(2,1)S(1)}, u32[]{:S(2)}, u32[]{:S(2)}) collective-permute-start(bf16[400,1024]{1,0:T(8,128)(2,1)S(1)} %collective-permute-done.4.args_0_.args_1_), channel_id=1, source_target_pairs={{0,32},{1,33},{2,34},{3,35},{4,36},{5,37},{6,38},{7,39},{8,40},{9,... | collective-permute-start | bytes 2457608 | tf_op jit(solution)/shard_map/ppermute | solution.py:28
  37.4 23.3 %collective-permute-start.7 = (bf16[400,1024]{1,0:T(8,128)(2,1)S(1)}, bf16[400,1024]{1,0:T(8,128)(2,1)S(1)}, u32[]{:S(2)}, u32[]{:S(2)}) collective-permute-start(bf16[400,1024]{1,0:T(8,128)(2,1)S(1)} %collective-permute-done.6.args_0_.args_3_), channel_id=1, source_target_pairs={{0,32},{1,33},{2,34},{3,35},{4,36},{5,37},{6,38},{7,39},{8,40},{9,... | collective-permute-start | bytes 2457608 | tf_op jit(solution)/shard_map/ppermute | solution.py:28
  46.7 22.2 %collective-permute-start.11 = (bf16[400,1024]{1,0:T(8,128)(2,1)S(1)}, bf16[400,1024]{1,0:T(8,128)(2,1)S(1)}, u32[]{:S(2)}, u32[]{:S(2)}) collective-permute-start(bf16[400,1024]{1,0:T(8,128)(2,1)S(1)} %collective-permute-done.10.args_0_.args_5_.both), channel_id=1, source_target_pairs={{0,32},{1,33},{2,34},{3,35},{4,36},{5,37},{6,38},{7,39},{8,40},{9,... | collective-permute-start | bytes 2457608 | tf_op jit(solution)/shard_map/ppermute | solution.py:28
  51.1 22.1 %collective-permute-start.13 = (bf16[400,1024]{1,0:T(8,128)(2,1)S(1)}, bf16[400,1024]{1,0:T(8,128)(2,1)S(1)}, u32[]{:S(2)}, u32[]{:S(2)}) collective-permute-start(bf16[400,1024]{1,0:T(8,128)(2,1)S(1)} %slice.9), channel_id=1, source_target_pairs={{0,3},{1,0},{2,1},{3,2},{4,7},{5,4},{6,5},{7,6},{8,11},{9,8},{10,9... | collective-permute-start | bytes 2457608 | tf_op jit(solution)/shard_map/ppermute | solution.py:28
  53.7 19.5 %collective-permute-start.12 = (bf16[384,1024]{1,0:T(8,128)(2,1)S(1)}, bf16[384,1024]{1,0:T(8,128)(2,1)S(1)}, u32[]{:S(2)}, u32[]{:S(2)}) collective-permute-start(bf16[384,1024]{1,0:T(8,128)(2,1)S(1)} %slice.8), channel_id=1, source_target_pairs={{0,1},{1,2},{2,3},{3,0},{4,5},{5,6},{6,7},{7,4},{8,9},{9,10},{10,1... | collective-permute-start | bytes 2359304 | tf_op jit(solution)/shard_map/ppermute | solution.py:28
  59.0 7.4 %collective-permute-start.14 = (bf16[208,1024]{1,0:T(8,128)(2,1)S(1)}, bf16[208,1024]{1,0:T(8,128)(2,1)S(1)}, u32[]{:S(2)}, u32[]{:S(2)}) collective-permute-start(bf16[208,1024]{1,0:T(8,128)(2,1)S(1)} %pick.1), channel_id=1, source_target_pairs={{0,4},{1,5},{2,6},{3,7},{4,8},{5,9},{6,10},{7,11},{8,12},{9,13},{1... | collective-permute-start | bytes 1277960 | tf_op jit(solution)/shard_map/ppermute | solution.py:28
  66.3 13.1 %collective-permute-start.15 = (bf16[208,1024]{1,0:T(8,128)(2,1)S(1)}, bf16[208,1024]{1,0:T(8,128)(2,1)S(1)}, u32[]{:S(2)}, u32[]{:S(2)}) collective-permute-start(bf16[208,1024]{1,0:T(8,128)(2,1)S(1)} %collective-permute-done.14.args_0_), channel_id=1, source_target_pairs={{0,32},{1,33},{2,34},{3,35},{4,36},{5,37},{6,38},{7,39},{8,40},{9,... | collective-permute-start | bytes 1277960 | tf_op jit(solution)/shard_map/ppermute | solution.py:28

commit v2 on v1

v2 whole, which is shorter than its diff:
```python
import jax
import jax.numpy as jnp
import numpy as np
from jax import lax
from jax.experimental import pallas as pl
from jax.experimental.pallas import tpu as pltpu
from jax.sharding import Mesh, PartitionSpec as P

AXES = ("x", "core", "z", "y")
SIZES = (4, 2, 8, 4)
ROWS = 192
WEIGHT = 1
KEYS = 16
DIM = 1024
VMEM = pl.BlockSpec(memory_space=pltpu.VMEM)
HBM = pl.BlockSpec(memory_space=pltpu.HBM)
SMEM = pl.BlockSpec(memory_space=pltpu.SMEM)


def permutation(move):
    pairs = []
    for source in np.ndindex(*SIZES):
        target = np.array(move(*source)) % np.array(SIZES)
        pairs.append((int(np.ravel_multi_index(source, SIZES)), int(np.ravel_multi_index(tuple(target), SIZES))))
    return pairs


def send(array, move, name):
    with jax.named_scope(name):
        return lax.ppermute(array, AXES, permutation(move))


def call(body, outs, scratch=(), flops=0, spaces=None, count=0, name=None, vmem=10):
    return pl.pallas_call(
        body,
        out_shape=outs,
        in_specs=spaces or [VMEM] * count,
        out_specs=VMEM if isinstance(outs, jax.ShapeDtypeStruct) else [VMEM] * len(outs),
        scratch_shapes=list(scratch),
        compiler_params=pltpu.CompilerParams(vmem_limit_bytes=vmem << 20),
        cost_estimate=pl.CostEstimate(flops=flops, bytes_accessed=0, transcendentals=0),
        name=name,
    )


def column_to_row(column):
    n = column.shape[0]
    diagonal = lax.broadcasted_iota(jnp.int32, (n, n), 0) == lax.broadcasted_iota(jnp.int32, (n, n), 1)
    return jnp.sum(jnp.where(diagonal, column, 0.0), axis=0, keepdims=True)


def normalise_body(_, sketches_hbm, labels_hbm, ranks_hbm, out, sketches, labels, ranks, sems):
    pairs = ((sketches_hbm, sketches), (labels_hbm, labels), (ranks_hbm, ranks))
    copies = [pltpu.make_async_copy(source, target, sems.at[i]) for i, (source, target) in enumerate(pairs)]
    for copy in copies:
        copy.start()
    for copy in copies[1:]:
        copy.wait()
    label_row = column_to_row(labels[...].astype(jnp.float32))
    rank_row = ranks[...]
    high = (rank_row // 256).astype(jnp.float32)
    low = (rank_row % 256).astype(jnp.float32)
    index = lax.broadcasted_iota(jnp.int32, (KEYS, ROWS), 0)
    rows = jnp.where(index == 0, label_row, jnp.where(index == 1, high, jnp.where(index == 2, low, 0.0)))
    out[ROWS : ROWS + KEYS, :] = jnp.zeros((KEYS, DIM), jnp.bfloat16)
    out[ROWS : ROWS + KEYS, 0:ROWS] = rows.astype(jnp.bfloat16)
    copies[0].wait()
    values = sketches[...]
    scale = lax.rsqrt(jnp.sum(values * values, axis=1, keepdims=True) + 1e-06)
    out[0:ROWS, :] = (values * scale).astype(jnp.bfloat16)


def count_of(block):
    return block.shape[0] // ROWS


def key_of(rows):
    return rows[0:1] * 65536.0 + rows[1:2] * 256.0 + rows[2:3]


def join_body(*refs):
    out, columns, start = refs[-1], [], 0
    for ref in refs[:-1]:
        size = count_of(ref) * ROWS
        out[start : start + size, :] = ref[0:size, :]
        width = -(-size // 128) * 128
        keys = ref[size : size + KEYS, 0:width].astype(jnp.float32)[0:8]
        columns.append(jnp.transpose(keys)[0:size])
        start += size
    rows = jnp.transpose(jnp.concatenate(columns, axis=0))
    out[start : start + KEYS, :] = jnp.zeros((KEYS, DIM), jnp.bfloat16)
    out[start : start + KEYS, 0:start] = jnp.concatenate([rows, jnp.zeros_like(rows)], axis=0).astype(jnp.bfloat16)


def join(name, *blocks, flops=0):
    total = sum(count_of(b) for b in blocks)
    shape = jax.ShapeDtypeStruct((total * ROWS + KEYS, DIM), jnp.bfloat16)
    return call(join_body, shape, count=len(blocks), flops=flops, name=name)(*blocks)


def highest(first, *rest):
    for rows in rest:
        first = jnp.maximum(first, rows)
    return first


def after_kernel(arrays, token):
    return lax.optimization_barrier((*arrays, token))[:-1]


def score(queries, bundles, name, token=None, weight=1):
    refs, layout = [], []
    for bundle in bundles:
        layout.append(len(bundle))
        refs += bundle
    blocks = [count_of(q) for q in queries]
    total, length = sum(blocks), 4 * ROWS
    halved = 2 in layout

    def body(*args):
        args = list(args)
        joined = args.pop() if halved else None
        if token is not None:
            args.pop(0)
        q_refs, k_refs, out = args[: len(queries)], args[len(queries) : -1], args[-1]
        parts = []
        for n in layout:
            if n == 1:
                whole = k_refs[0]
                key_rows = whole[length : length + KEYS, 0:length]
            else:
                top, bottom = k_refs[:2]
                joined[0 : length // 2, :] = top[0 : length // 2, :]
                joined[length // 2 : length, :] = bottom[0 : length // 2, :]
                whole = joined
                key_rows = bottom[length // 2 : length // 2 + KEYS, 0:length]
            k_refs = k_refs[n:]
            key = key_of(key_rows.astype(jnp.float32)[0:8])
            parts += [(whole, start, key[:, start : start + 256]) for start in range(0, length, 256)]
        row = 0
        for q_ref, count in zip(q_refs, blocks):
            size = count * ROWS
            key_row = key_of(q_ref[size : size + KEYS, 0:size].astype(jnp.float32)[0:8])
            key_q = jnp.transpose(jnp.broadcast_to(key_row, (8, size)))[:, 0:1]
            base = jnp.floor(key_q * (1.0 / 65536.0)) * 65536.0
            best = jnp.full((size, 128), -1.0, jnp.float32)
            for ref, start, key_k in parts:
                scores = lax.dot_general(
                    q_ref[0:size, :], ref[start : start + 256, :], (((1,), (1,)), ((), ())), preferred_element_type=jnp.float32
                )
                allowed = (key_k < key_q) & (key_k >= base)
                scores = jnp.where(allowed, scores, -1.0)
                best = jnp.maximum(best, jnp.maximum(scores[:, 0:128], scores[:, 128:256]))
            top = jnp.max(best, axis=1, keepdims=True)
            for i in range(count):
                out[row : row + 1, :] = column_to_row(top[i * ROWS : (i + 1) * ROWS])
                row += 1

    flops = int(2 * DIM * ROWS * ROWS * total * 4 * len(bundles) * weight * WEIGHT)
    operands = ([] if token is None else [token]) + list(queries) + refs
    return call(
        body,
        jax.ShapeDtypeStruct((total, ROWS), jnp.float32),
        scratch=[pltpu.VMEM((length, DIM), jnp.bfloat16)] if halved else [],
        flops=flops,
        count=len(operands),
        name=name,
    )(*operands)


def on_device(sketches, labels, ranks):
    core = lax.axis_index("core").astype(jnp.int32)
    z = lax.axis_index("z").astype(jnp.int32)
    place = jnp.stack([core, z])
    own = call(
        normalise_body,
        jax.ShapeDtypeStruct((ROWS + KEYS, DIM), jnp.bfloat16),
        scratch=[
            pltpu.VMEM((ROWS, DIM), jnp.float32),
            pltpu.VMEM((ROWS, 1), jnp.int32),
            pltpu.VMEM((1, ROWS), jnp.int32),
            pltpu.SemaphoreType.DMA((3,)),
        ],
        spaces=[SMEM] + [HBM] * 3,
        name="normalise",
    )(place, sketches, labels, ranks.reshape(1, ROWS))

    def first(step):
        return lambda x, c, z, y: (x + step * (1 - c), c, z, y + step * c)

    def second(step):
        return lambda x, c, z, y: (x + step * c, c, z, y + step * (1 - c))

    def along_z(x, c, z, y):
        return (x, c, z + 1 - 2 * c, y)

    def across(x, c, z, y):
        return (x, c + 1, z, y)

    half = 2 * ROWS
    partner = send(own, across, "partner")
    line = [send(own, first(2), "key_far"), send(own, first(1), "key_up"), send(own, first(-1), "key_down")]
    here = join("here", own, partner, flops=4 << 30)
    r1 = send(here, along_z, "r1")
    bundle = join("bundle", own, *line)
    after, before = send(bundle, second(-1), "bundle_down"), send(bundle, second(1), "bundle_up")
    s0 = score([here], [[bundle]], "s0", weight=10)
    (r1,) = after_kernel([r1], s0)
    r2, e1 = send(r1, along_z, "r2"), send(r1, across, "e1")
    s1 = score([r1, e1], [[bundle]], "s1")
    (r2,) = after_kernel([r2], s1)
    r3, e2 = send(r2, along_z, "r3"), send(r2, across, "e2")
    after, before, r2 = after_kernel([after, before, r2], r2)
    opposite = [send(before[0 : half + KEYS], second(1), "opposite_up"), send(after[half:], second(-1), "opposite_down")]
    s2 = score([here, r1, e1], [[after], [before]], "s2")
    (r3,) = after_kernel([r3], s2)
    r4, e3 = send(r3, along_z, "r4"), send(r3, across, "e3")
    s3 = score([r2, e2], [[bundle], [after], [before]], "s3", r3)
    opposite = after_kernel(opposite, s3)
    s4 = score([r3, e3], [[bundle], [after], [before], opposite], "s4")
    s5 = score([here, r1, e1, r2, e2], [opposite], "s5", s4)
    (r4,) = after_kernel([r4], s5)
    s6 = score([r4], [[bundle], [after], [before], opposite], "s6")

    def merge_body(at, s0, s1, s2, s3, s4, s5, s6, out):
        me, level = at[0], at[1]
        sign = 2 * me - 1
        two, five = s2[...], s5[...]
        groups = (
            highest(s0[...], two[0:2], five[0:2]),
            highest(s1[...], two[2:6], five[2:6]),
            highest(s3[...], five[6:10]),
            s4[...],
            s6[...],
        )
        for k, rows in enumerate(groups):
            for j in range(rows.shape[0]):
                which = me if j in (0, 3) else 1 - me
                step = k if k in (0, 4) else (sign * k if j < 2 else -sign * k)
                out[pl.ds(which * 8 + lax.rem(level + step + 16, 8), 1), :] = rows[j : j + 1]

    scores = (s0, s1, s2, s3, s4, s5, s6)
    partial = call(
        merge_body, jax.ShapeDtypeStruct((16, ROWS), jnp.float32), spaces=[SMEM] + [VMEM] * len(scores), name="merge"
    )(place, *scores)
    returned = lax.all_to_all(partial, ("core", "z"), split_axis=0, concat_axis=0, tiled=True)
    return jnp.max(returned, axis=0)


def solution(mesh):
    fine = Mesh(mesh.devices.reshape(SIZES), AXES)
    return jax.shard_map(
        on_device,
        mesh=fine,
        in_specs=(P(AXES, None), P(AXES, None), P(AXES)),
        out_specs=P(AXES),
        check_vma=False,
    )
```

time: 98.1 us -> 87.9 us (0.90)
  waiting for transfers between devices: 22.4 us -> 16.3 us
  Pallas kernels: 28.7 us -> 26 us
  blocking collectives: 12.8 us -> 10.8 us
    ppermute x16 -> x15, waiting for transfers between devices: 22.4 us -> 16.3 us  [send(): return lax.ppermute(array, AXES, permutation(move))]
    pallas_call x12 -> x10, Pallas kernels: 28.1 us -> 25.4 us  [the longest x7 23.9 us: score(): call(body, jax.ShapeDtypeStruct((total, ROWS), jnp.float32), scratch=[plt...]
    all_to_all x1, blocking collectives: 12.8 us -> 10.8 us  [on_device(): lax.all_to_all(partial, ('core', 'z'), split_axis=0, concat_axis=0, tiled...]
    ppermute x16 -> x15, starting transfers between devices: 30.4 us -> 31.1 us  [send(): return lax.ppermute(array, AXES, permutation(move))]
  transfers between devices with their start and end apart: 16 -> 15, of which waited for: 6 -> 6; matrix products, arithmetic and copies ran while one was open for 0% -> 0% of each run, Pallas kernels for 23% -> 24%
where the time goes in v2:
time: 87.9 us; the launch traced here: 87.7 us
  starting transfers between devices  31.1 us (35%)
  Pallas kernels  26 us (30%)
  waiting for transfers between devices  16.3 us (19%)
  blocking collectives  10.8 us (12%)
  local copies, waits for them, and re-layouts  2.73 us (3%)
    ppermute x15, starting transfers between devices, send(): return lax.ppermute(array, AXES, permutation(move))  31.1 us
    pallas_call x7, Pallas kernels, score(): call(body, jax.ShapeDtypeStruct((total, ROWS), jnp.float32), scratch=[plt...  23.9 us
    ppermute x15, waiting for transfers between devices, send(): return lax.ppermute(array, AXES, permutation(move))  16.3 us
    all_to_all x1, blocking collectives, on_device(): lax.all_to_all(partial, ('core', 'z'), split_axis=0, concat_axis=0, tiled...  10.8 us
    unnamed x5, local copies, waits for them, and re-layouts  2.6 us
  transfers between devices with their start and end apart: 15, of which 6 were waited for; matrix products, arithmetic and copies ran while one was open for 0% of the time, Pallas kernels for 24%

profile of v2, /device:TPU:1, one launch (start us, length us, event | category | flops | bytes accessed | tf_op | source)
XLA Modules:
  0.0 87.7 jit_solution(6806959457199345908)
XLA Ops:
  0.9 1.1 %copy-done = f32[192,1024]{1,0:T(8,128)S(1)} copy-done((f32[192,1024]{1,0:T(8,128)S(1)}, f32[192,1024]{1,0:T(8,128)}, u32[]{:S(2)}) %copy-start) | copy-done | bytes 786456
  2.7 1.0 %normalise.1.refs_0_ = bf16[208,1024]{1,0:T(8,128)(2,1)S(1)} custom-call(s32[2]{0:T(128)S(1)} %pad_add_fusion._.at, f32[192,1024]{1,0:T(8,128)S(1)} %copy-done, s32[192,1]{1,0:T(8,128)S(1)} %copy.5.labels_hbm, s32[1,192]{1,0:T(1,128)S(1)} %bitcast.5), custom_call_target="tpu_custom_call" | custom-call | tf_op jit(solution)/shard_map/normalise/pallas_call | solution.py:175
  3.7 3.3 %collective-permute-start = (bf16[208,1024]{1,0:T(8,128)(2,1)S(1)}, bf16[208,1024]{1,0:T(8,128)(2,1)S(1)}, u32[]{:S(2)}, u32[]{:S(2)}) collective-permute-start(bf16[208,1024]{1,0:T(8,128)(2,1)S(1)} %normalise.1.refs_0_), channel_id=1, source_target_pairs={{0,32},{1,33},{2,34},{3,35},{4,36},{5,37},{6,38},{7,39},{8,40},{9,... | collective-permute-start | bytes 1277960 | tf_op jit(solution)/shard_map/partner/ppermute | solution.py:30
  7.0 1.2 %collective-permute-start.1 = (bf16[208,1024]{1,0:T(8,128)(2,1)S(1)}, bf16[208,1024]{1,0:T(8,128)(2,1)S(1)}, u32[]{:S(2)}, u32[]{:S(2)}) collective-permute-start(bf16[208,1024]{1,0:T(8,128)(2,1)S(1)} %normalise.1.refs_0_), channel_id=1, source_target_pairs={{0,128},{1,129},{2,130},{3,131},{4,132},{5,133},{6,134},{7,135},{8... | collective-permute-start | bytes 1277960 | tf_op jit(solution)/shard_map/key_far/ppermute | solution.py:30
  8.6 2.3 %collective-permute-start.3 = (bf16[208,1024]{1,0:T(8,128)(2,1)S(1)}, bf16[208,1024]{1,0:T(8,128)(2,1)S(1)}, u32[]{:S(2)}, u32[]{:S(2)}) collective-permute-start(bf16[208,1024]{1,0:T(8,128)(2,1)S(1)} %normalise.1.refs_0_), channel_id=1, source_target_pairs={{0,192},{1,193},{2,194},{3,195},{4,196},{5,197},{6,198},{7,199},{8... | collective-permute-start | bytes 1277960 | tf_op jit(solution)/shard_map/key_down/ppermute | solution.py:30
  11.1 5.6 %collective-permute-start.4 = (bf16[400,1024]{1,0:T(8,128)(2,1)S(1)}, bf16[400,1024]{1,0:T(8,128)(2,1)S(1)}, u32[]{:S(2)}, u32[]{:S(2)}) collective-permute-start(bf16[400,1024]{1,0:T(8,128)(2,1)S(1)} %here.1.args_0_.args_1_), channel_id=1, source_target_pairs={{0,4},{1,5},{2,6},{3,7},{4,8},{5,9},{6,10},{7,11},{8,12},{9,13},{1... | collective-permute-start | bytes 2457608 | tf_op jit(solution)/shard_map/r1/ppermute | solution.py:30
  16.7 3.6 %collective-permute-done.2.refs_2_ = bf16[208,1024]{1,0:T(8,128)(2,1)S(1)} collective-permute-done((bf16[208,1024]{1,0:T(8,128)(2,1)S(1)}, bf16[208,1024]{1,0:T(8,128)(2,1)S(1)}, u32[]{:S(2)}, u32[]{:S(2)}) %collective-permute-start.2) | collective-permute-done | bytes 426016 | tf_op jit(solution)/shard_map/key_up/ppermute | solution.py:30
  20.6 1.2 %collective-permute-start.6 = (bf16[784,1024]{1,0:T(8,128)(2,1)S(1)}, bf16[784,1024]{1,0:T(8,128)(2,1)S(1)}, u32[]{:S(2)}, u32[]{:S(2)}) collective-permute-start(bf16[784,1024]{1,0:T(8,128)(2,1)S(1)} %bundle.1.args_1_.args_2_.args_3_), channel_id=1, source_target_pairs={{0,3},{1,0},{2,1},{3,2},{4,7},{5,4},{6,5},{7,6},{8,11},{9,8},{10,9... | collective-permute-start | bytes 4816904 | tf_op jit(solution)/shard_map/bundle_down/ppermute | solution.py:30
  23.1 2.9 %collective-permute-done.4.args_0_.args_1_.args_2_ = bf16[400,1024]{1,0:T(8,128)(2,1)S(1)} collective-permute-done((bf16[400,1024]{1,0:T(8,128)(2,1)S(1)}, bf16[400,1024]{1,0:T(8,128)(2,1)S(1)}, u32[]{:S(2)}, u32[]{:S(2)}) %collective-permute-start.4) | collective-permute-done | bytes 819232 | tf_op jit(solution)/shard_map/r1/ppermute | solution.py:30
  26.0 2.1 %collective-permute-start.5 = (bf16[400,1024]{1,0:T(8,128)(2,1)S(1)}, bf16[400,1024]{1,0:T(8,128)(2,1)S(1)}, u32[]{:S(2)}, u32[]{:S(2)}) collective-permute-start(bf16[400,1024]{1,0:T(8,128)(2,1)S(1)} %collective-permute-done.4.args_0_.args_1_.args_2_), channel_id=1, source_target_pairs={{0,32},{1,33},{2,34},{3,35},{4,36},{5,37},{6,38},{7,39},{8,40},{9,... | collective-permute-start | bytes 2457608 | tf_op jit(solution)/shard_map/e1/ppermute | solution.py:30
  28.1 1.7 %collective-permute-start.8 = (bf16[400,1024]{1,0:T(8,128)(2,1)S(1)}, bf16[400,1024]{1,0:T(8,128)(2,1)S(1)}, u32[]{:S(2)}, u32[]{:S(2)}) collective-permute-start(bf16[400,1024]{1,0:T(8,128)(2,1)S(1)} %collective-permute-done.4.args_0_.args_1_.args_2_), channel_id=1, source_target_pairs={{0,4},{1,5},{2,6},{3,7},{4,8},{5,9},{6,10},{7,11},{8,12},{9,13},{1... | collective-permute-start | bytes 2457608 | tf_op jit(solution)/shard_map/r2/ppermute | solution.py:30
  30.1 1.7 %s1_.1.s1 = f32[4,192]{1,0:T(4,128)S(1)} custom-call(bf16[400,1024]{1,0:T(8,128)(2,1)S(1)} %collective-permute-done.4.args_0_.args_1_.args_2_, bf16[400,1024]{1,0:T(8,128)(2,1)S(1)} %collective-permute-done.5.args_1_.args_2_.args_3_, bf16[784,1024]{1,0:T(8,128)(2,1)S(1)} %bundle.1.args_1_.args_2_.args_3_), custom_call_target="tpu_custom_call" | custom-call | flops 1207959552 | tf_op jit(solution)/shard_map/s1/pallas_call | solution.py:161
  31.7 7.8 %collective-permute-done.8.args_1_.args_4_ = bf16[400,1024]{1,0:T(8,128)(2,1)S(1)} collective-permute-done((bf16[400,1024]{1,0:T(8,128)(2,1)S(1)}, bf16[400,1024]{1,0:T(8,128)(2,1)S(1)}, u32[]{:S(2)}, u32[]{:S(2)}) %collective-permute-start.8) | collective-permute-done | bytes 819232 | tf_op jit(solution)/shard_map/r2/ppermute | solution.py:30
  39.6 3.0 %collective-permute-start.9 = (bf16[400,1024]{1,0:T(8,128)(2,1)S(1)}, bf16[400,1024]{1,0:T(8,128)(2,1)S(1)}, u32[]{:S(2)}, u32[]{:S(2)}) collective-permute-start(bf16[400,1024]{1,0:T(8,128)(2,1)S(1)} %collective-permute-done.8.args_1_.args_4_), channel_id=1, source_target_pairs={{0,4},{1,5},{2,6},{3,7},{4,8},{5,9},{6,10},{7,11},{8,12},{9,13},{1... | collective-permute-start | bytes 2457608 | tf_op jit(solution)/shard_map/r3/ppermute | solution.py:30
  43.8 2.3 %collective-permute-start.13 = (bf16[400,1024]{1,0:T(8,128)(2,1)S(1)}, bf16[400,1024]{1,0:T(8,128)(2,1)S(1)}, u32[]{:S(2)}, u32[]{:S(2)}) collective-permute-start(bf16[400,1024]{1,0:T(8,128)(2,1)S(1)} %slice.7), channel_id=1, source_target_pairs={{0,3},{1,0},{2,1},{3,2},{4,7},{5,4},{6,5},{7,6},{8,11},{9,8},{10,9... | collective-permute-start | bytes 2457608 | tf_op jit(solution)/shard_map/opposite_down/ppermute | solution.py:30
  46.1 4.4 %s2_.1.s2 = f32[6,192]{1,0:T(8,128)S(1)} custom-call(bf16[400,1024]{1,0:T(8,128)(2,1)S(1)} %here.1.args_0_.args_1_, bf16[400,1024]{1,0:T(8,128)(2,1)S(1)} %collective-permute-done.4.args_0_.args_1_.args_2_, bf16[400,1024]{1,0:T(8,128)(2,1)S(1)} %collective-permute-done.5.args_1_.args_2_.args_3_, ...), custom_call_target="tpu_custom_call" | custom-call | flops 3623878656 | tf_op jit(solution)/shard_map/s2/pallas_call | solution.py:161
  50.5 1.3 %collective-permute-done.9.args_0_ = bf16[400,1024]{1,0:T(8,128)(2,1)S(1)} collective-permute-done((bf16[400,1024]{1,0:T(8,128)(2,1)S(1)}, bf16[400,1024]{1,0:T(8,128)(2,1)S(1)}, u32[]{:S(2)}, u32[]{:S(2)}) %collective-permute-start.9) | collective-permute-done | bytes 819232 | tf_op jit(solution)/shard_map/r3/ppermute | solution.py:30
  51.8 3.4 %collective-permute-start.11 = (bf16[400,1024]{1,0:T(8,128)(2,1)S(1)}, bf16[400,1024]{1,0:T(8,128)(2,1)S(1)}, u32[]{:S(2)}, u32[]{:S(2)}) collective-permute-start(bf16[400,1024]{1,0:T(8,128)(2,1)S(1)} %collective-permute-done.9.args_0_), channel_id=1, source_target_pairs={{0,32},{1,33},{2,34},{3,35},{4,36},{5,37},{6,38},{7,39},{8,40},{9,... | collective-permute-start | bytes 2457608 | tf_op jit(solution)/shard_map/e3/ppermute | solution.py:30
  55.2 3.6 %collective-permute-start.14 = (bf16[400,1024]{1,0:T(8,128)(2,1)S(1)}, bf16[400,1024]{1,0:T(8,128)(2,1)S(1)}, u32[]{:S(2)}, u32[]{:S(2)}) collective-permute-start(bf16[400,1024]{1,0:T(8,128)(2,1)S(1)} %collective-permute-done.9.args_0_), channel_id=1, source_target_pairs={{0,4},{1,5},{2,6},{3,7},{4,8},{5,9},{6,10},{7,11},{8,12},{9,13},{1... | collective-permute-start | bytes 2457608 | tf_op jit(solution)/shard_map/r4/ppermute | solution.py:30
  58.8 4.4 %s3.1 = f32[4,192]{1,0:T(4,128)S(1)} custom-call(bf16[400,1024]{1,0:T(8,128)(2,1)S(1)} %collective-permute-done.9.args_0_, bf16[400,1024]{1,0:T(8,128)(2,1)S(1)} %collective-permute-done.8.args_1_.args_4_, bf16[400,1024]{1,0:T(8,128)(2,1)S(1)} %collective-permute-done.10.args_2_.args_5_, bf16[784,1024]{1,0:T(8,128)(2,1)S(1)} %bundle.1.args_1_.args_2_.args_3_, ...), custom_call_target="tpu_custom_call" | custom-call | flops 3623878656 | tf_op jit(solution)/shard_map/s3/pallas_call | solution.py:161
  63.2 5.8 %s4_.1.args_0_.s4 = f32[4,192]{1,0:T(4,128)S(1)} custom-call(bf16[400,1024]{1,0:T(8,128)(2,1)S(1)} %collective-permute-done.9.args_0_, bf16[400,1024]{1,0:T(8,128)(2,1)S(1)} %collective-permute-done.11.args_1_, bf16[784,1024]{1,0:T(8,128)(2,1)S(1)} %bundle.1.args_1_.args_2_.args_3_, bf16[784,1024]{1,0:T(8,128)(2,1)S(1)} %collective-permute-done.6.args_3_.args_4_.args_2_, ...), custom_call_target="tpu_custom_call" | custom-call | flops 4831838208 | tf_op jit(solution)/shard_map/s4/pallas_call | solution.py:161
  69.0 3.7 %s5.1 = f32[10,192]{1,0:T(8,128)S(1)} custom-call(f32[4,192]{1,0:T(4,128)S(1)} %s4_.1.args_0_.s4, bf16[400,1024]{1,0:T(8,128)(2,1)S(1)} %here.1.args_0_.args_1_, bf16[400,1024]{1,0:T(8,128)(2,1)S(1)} %collective-permute-done.4.args_0_.args_1_.args_2_, bf16[400,1024]{1,0:T(8,128)(2,1)S(1)} %collective-permute-done.5.args_1_.args_2_.args_3_, ...), custom_call_target="tpu_custom_call" | custom-call | flops 3019898880 | tf_op jit(solution)/shard_map/s5/pallas_call | solution.py:161
  72.7 3.0 %s6.1 = f32[2,192]{1,0:T(2,128)S(1)} custom-call(bf16[400,1024]{1,0:T(8,128)(2,1)S(1)} %collective-permute-done.14.args_0_, bf16[784,1024]{1,0:T(8,128)(2,1)S(1)} %bundle.1.args_1_.args_2_.args_3_, bf16[784,1024]{1,0:T(8,128)(2,1)S(1)} %collective-permute-done.6.args_3_.args_4_.args_2_, bf16[784,1024]{1,0:T(8,128)(2,1)S(1)} %collective-permute-done.7.args_4_.args_5_.args_3_, ...), custom_call_target="tpu_custom_call" | custom-call | flops 2415919104 | tf_op jit(solution)/shard_map/s6/pallas_call | solution.py:161
  76.3 10.8 %all_to_all.9 = f32[16,1,192]{2,1,0:T(1,128)S(1)} all-to-all(f32[16,1,192]{2,1,0:T(1,128)S(1)} %copy.6), channel_id=1, replica_groups=mesh['x'=4,'core'=2,'z'=8,'y'=4] {'core','z'}, dimensions={0} | all-to-all | bytes 24576 | tf_op jit(solution)/shard_map/all_to_all | solution.py:246
  (28 shorter events, 6.4 us)
Async XLA Ops:
  0.9 1.1 %copy-start = (f32[192,1024]{1,0:T(8,128)S(1)}, f32[192,1024]{1,0:T(8,128)}, u32[]{:S(2)}) copy-start(f32[192,1024]{1,0:T(8,128)} %sketches_hbm.1) | copy-start | bytes 2359300
  2.0 0.7 copy-start.1
  3.7 7.2 %collective-permute-start = (bf16[208,1024]{1,0:T(8,128)(2,1)S(1)}, bf16[208,1024]{1,0:T(8,128)(2,1)S(1)}, u32[]{:S(2)}, u32[]{:S(2)}) collective-permute-start(bf16[208,1024]{1,0:T(8,128)(2,1)S(1)} %normalise.1.refs_0_), channel_id=1, source_target_pairs={{0,32},{1,33},{2,34},{3,35},{4,36},{5,37},{6,38},{7,39},{8,40},{9,... | collective-permute-start | bytes 1277960 | tf_op jit(solution)/shard_map/partner/ppermute | solution.py:30
  7.0 9.7 %collective-permute-start.1 = (bf16[208,1024]{1,0:T(8,128)(2,1)S(1)}, bf16[208,1024]{1,0:T(8,128)(2,1)S(1)}, u32[]{:S(2)}, u32[]{:S(2)}) collective-permute-start(bf16[208,1024]{1,0:T(8,128)(2,1)S(1)} %normalise.1.refs_0_), channel_id=1, source_target_pairs={{0,128},{1,129},{2,130},{3,131},{4,132},{5,133},{6,134},{7,135},{8... | collective-permute-start | bytes 1277960 | tf_op jit(solution)/shard_map/key_far/ppermute | solution.py:30
  8.2 12.2 %collective-permute-start.2 = (bf16[208,1024]{1,0:T(8,128)(2,1)S(1)}, bf16[208,1024]{1,0:T(8,128)(2,1)S(1)}, u32[]{:S(2)}, u32[]{:S(2)}) collective-permute-start(bf16[208,1024]{1,0:T(8,128)(2,1)S(1)} %normalise.1.refs_0_), channel_id=1, source_target_pairs={{0,64},{1,65},{2,66},{3,67},{4,68},{5,69},{6,70},{7,71},{8,72},{9,... | collective-permute-start | bytes 1277960 | tf_op jit(solution)/shard_map/key_up/ppermute | solution.py:30
  8.6 11.8 %collective-permute-start.3 = (bf16[208,1024]{1,0:T(8,128)(2,1)S(1)}, bf16[208,1024]{1,0:T(8,128)(2,1)S(1)}, u32[]{:S(2)}, u32[]{:S(2)}) collective-permute-start(bf16[208,1024]{1,0:T(8,128)(2,1)S(1)} %normalise.1.refs_0_), channel_id=1, source_target_pairs={{0,192},{1,193},{2,194},{3,195},{4,196},{5,197},{6,198},{7,199},{8... | collective-permute-start | bytes 1277960 | tf_op jit(solution)/shard_map/key_down/ppermute | solution.py:30
  11.1 14.9 %collective-permute-start.4 = (bf16[400,1024]{1,0:T(8,128)(2,1)S(1)}, bf16[400,1024]{1,0:T(8,128)(2,1)S(1)}, u32[]{:S(2)}, u32[]{:S(2)}) collective-permute-start(bf16[400,1024]{1,0:T(8,128)(2,1)S(1)} %here.1.args_0_.args_1_), channel_id=1, source_target_pairs={{0,4},{1,5},{2,6},{3,7},{4,8},{5,9},{6,10},{7,11},{8,12},{9,13},{1... | collective-permute-start | bytes 2457608 | tf_op jit(solution)/shard_map/r1/ppermute | solution.py:30
  20.6 21.9 %collective-permute-start.6 = (bf16[784,1024]{1,0:T(8,128)(2,1)S(1)}, bf16[784,1024]{1,0:T(8,128)(2,1)S(1)}, u32[]{:S(2)}, u32[]{:S(2)}) collective-permute-start(bf16[784,1024]{1,0:T(8,128)(2,1)S(1)} %bundle.1.args_1_.args_2_.args_3_), channel_id=1, source_target_pairs={{0,3},{1,0},{2,1},{3,2},{4,7},{5,4},{6,5},{7,6},{8,11},{9,8},{10,9... | collective-permute-start | bytes 4816904 | tf_op jit(solution)/shard_map/bundle_down/ppermute | solution.py:30
  21.8 21.1 %collective-permute-start.7 = (bf16[784,1024]{1,0:T(8,128)(2,1)S(1)}, bf16[784,1024]{1,0:T(8,128)(2,1)S(1)}, u32[]{:S(2)}, u32[]{:S(2)}) collective-permute-start(bf16[784,1024]{1,0:T(8,128)(2,1)S(1)} %bundle.1.args_1_.args_2_.args_3_), channel_id=1, source_target_pairs={{0,1},{1,2},{2,3},{3,0},{4,5},{5,6},{6,7},{7,4},{8,9},{9,10},{10,1... | collective-permute-start | bytes 4816904 | tf_op jit(solution)/shard_map/bundle_up/ppermute | solution.py:30
  26.0 4.0 %collective-permute-start.5 = (bf16[400,1024]{1,0:T(8,128)(2,1)S(1)}, bf16[400,1024]{1,0:T(8,128)(2,1)S(1)}, u32[]{:S(2)}, u32[]{:S(2)}) collective-permute-start(bf16[400,1024]{1,0:T(8,128)(2,1)S(1)} %collective-permute-done.4.args_0_.args_1_.args_2_), channel_id=1, source_target_pairs={{0,32},{1,33},{2,34},{3,35},{4,36},{5,37},{6,38},{7,39},{8,40},{9,... | collective-permute-start | bytes 2457608 | tf_op jit(solution)/shard_map/e1/ppermute | solution.py:30
  28.1 11.5 %collective-permute-start.8 = (bf16[400,1024]{1,0:T(8,128)(2,1)S(1)}, bf16[400,1024]{1,0:T(8,128)(2,1)S(1)}, u32[]{:S(2)}, u32[]{:S(2)}) collective-permute-start(bf16[400,1024]{1,0:T(8,128)(2,1)S(1)} %collective-permute-done.4.args_0_.args_1_.args_2_), channel_id=1, source_target_pairs={{0,4},{1,5},{2,6},{3,7},{4,8},{5,9},{6,10},{7,11},{8,12},{9,13},{1... | collective-permute-start | bytes 2457608 | tf_op jit(solution)/shard_map/r2/ppermute | solution.py:30
  39.6 12.2 %collective-permute-start.9 = (bf16[400,1024]{1,0:T(8,128)(2,1)S(1)}, bf16[400,1024]{1,0:T(8,128)(2,1)S(1)}, u32[]{:S(2)}, u32[]{:S(2)}) collective-permute-start(bf16[400,1024]{1,0:T(8,128)(2,1)S(1)} %collective-permute-done.8.args_1_.args_4_), channel_id=1, source_target_pairs={{0,4},{1,5},{2,6},{3,7},{4,8},{5,9},{6,10},{7,11},{8,12},{9,13},{1... | collective-permute-start | bytes 2457608 | tf_op jit(solution)/shard_map/r3/ppermute | solution.py:30
  42.5 16.3 %collective-permute-start.10 = (bf16[400,1024]{1,0:T(8,128)(2,1)S(1)}, bf16[400,1024]{1,0:T(8,128)(2,1)S(1)}, u32[]{:S(2)}, u32[]{:S(2)}) collective-permute-start(bf16[400,1024]{1,0:T(8,128)(2,1)S(1)} %collective-permute-done.8.args_1_.args_4_), channel_id=1, source_target_pairs={{0,32},{1,33},{2,34},{3,35},{4,36},{5,37},{6,38},{7,39},{8,40},{9,... | collective-permute-start | bytes 2457608 | tf_op jit(solution)/shard_map/e2/ppermute | solution.py:30
  43.0 20.2 %collective-permute-start.12 = (bf16[400,1024]{1,0:T(8,128)(2,1)S(1)}, bf16[400,1024]{1,0:T(8,128)(2,1)S(1)}, u32[]{:S(2)}, u32[]{:S(2)}) collective-permute-start(bf16[400,1024]{1,0:T(8,128)(2,1)S(1)} %slice.6), channel_id=1, source_target_pairs={{0,1},{1,2},{2,3},{3,0},{4,5},{5,6},{6,7},{7,4},{8,9},{9,10},{10,1... | collective-permute-start | bytes 2457608 | tf_op jit(solution)/shard_map/opposite_up/ppermute | solution.py:30
  43.8 19.4 %collective-permute-start.13 = (bf16[400,1024]{1,0:T(8,128)(2,1)S(1)}, bf16[400,1024]{1,0:T(8,128)(2,1)S(1)}, u32[]{:S(2)}, u32[]{:S(2)}) collective-permute-start(bf16[400,1024]{1,0:T(8,128)(2,1)S(1)} %slice.7), channel_id=1, source_target_pairs={{0,3},{1,0},{2,1},{3,2},{4,7},{5,4},{6,5},{7,6},{8,11},{9,8},{10,9... | collective-permute-start | bytes 2457608 | tf_op jit(solution)/shard_map/opposite_down/ppermute | solution.py:30
  51.8 11.4 %collective-permute-start.11 = (bf16[400,1024]{1,0:T(8,128)(2,1)S(1)}, bf16[400,1024]{1,0:T(8,128)(2,1)S(1)}, u32[]{:S(2)}, u32[]{:S(2)}) collective-permute-start(bf16[400,1024]{1,0:T(8,128)(2,1)S(1)} %collective-permute-done.9.args_0_), channel_id=1, source_target_pairs={{0,32},{1,33},{2,34},{3,35},{4,36},{5,37},{6,38},{7,39},{8,40},{9,... | collective-permute-start | bytes 2457608 | tf_op jit(solution)/shard_map/e3/ppermute | solution.py:30
  55.2 17.5 %collective-permute-start.14 = (bf16[400,1024]{1,0:T(8,128)(2,1)S(1)}, bf16[400,1024]{1,0:T(8,128)(2,1)S(1)}, u32[]{:S(2)}, u32[]{:S(2)}) collective-permute-start(bf16[400,1024]{1,0:T(8,128)(2,1)S(1)} %collective-permute-done.9.args_0_), channel_id=1, source_target_pairs={{0,4},{1,5},{2,6},{3,7},{4,8},{5,9},{6,10},{7,11},{8,12},{9,13},{1... | collective-permute-start | bytes 2457608 | tf_op jit(solution)/shard_map/r4/ppermute | solution.py:30

commit v3 on v2

v3 whole, which is shorter than its diff:
```python
import jax
import jax.numpy as jnp
import numpy as np
from jax import lax
from jax.experimental import pallas as pl
from jax.experimental.pallas import tpu as pltpu
from jax.sharding import Mesh, PartitionSpec as P

AXES = ("x", "core", "z", "y")
SIZES = (4, 2, 8, 4)
ROWS = 192
WEIGHT = 1
W2, W3, W5, W6, W7 = 10, 10, 1, 1, 10
KEYS = 16
DIM = 1024
VMEM = pl.BlockSpec(memory_space=pltpu.VMEM)
SMEM = pl.BlockSpec(memory_space=pltpu.SMEM)


def permutation(move):
    pairs = []
    for source in np.ndindex(*SIZES):
        target = np.array(move(*source)) % np.array(SIZES)
        pairs.append((int(np.ravel_multi_index(source, SIZES)), int(np.ravel_multi_index(tuple(target), SIZES))))
    return pairs


def send(array, move, name):
    with jax.named_scope(name):
        return lax.ppermute(array, AXES, permutation(move))


def call(body, outs, scratch=(), flops=0, spaces=None, count=0, name=None, vmem=16):
    return pl.pallas_call(
        body,
        out_shape=outs,
        in_specs=spaces or [VMEM] * count,
        out_specs=VMEM if isinstance(outs, jax.ShapeDtypeStruct) else [VMEM] * len(outs),
        scratch_shapes=list(scratch),
        compiler_params=pltpu.CompilerParams(vmem_limit_bytes=vmem << 20),
        cost_estimate=pl.CostEstimate(flops=flops, bytes_accessed=0, transcendentals=0),
        name=name,
    )


def column_to_row(column):
    n = column.shape[0]
    diagonal = lax.broadcasted_iota(jnp.int32, (n, n), 0) == lax.broadcasted_iota(jnp.int32, (n, n), 1)
    return jnp.sum(jnp.where(diagonal, column, 0.0), axis=0, keepdims=True)


def normalise_body(_, sketches, labels, ranks, out):
    rank_row = ranks[...]
    high = (rank_row // 256).astype(jnp.float32)
    low = (rank_row % 256).astype(jnp.float32)
    index = lax.broadcasted_iota(jnp.int32, (KEYS, ROWS), 0)
    rows = jnp.where(index == 0, labels[...].astype(jnp.float32), jnp.where(index == 1, high, jnp.where(index == 2, low, 0.0)))
    out[ROWS : ROWS + KEYS, :] = jnp.zeros((KEYS, DIM), jnp.bfloat16)
    out[ROWS : ROWS + KEYS, 0:ROWS] = rows.astype(jnp.bfloat16)
    values = sketches[...]
    scale = lax.rsqrt(jnp.sum(values * values, axis=1, keepdims=True) + 1e-06)
    out[0:ROWS, :] = (values * scale).astype(jnp.bfloat16)


def count_of(block):
    return block.shape[0] // ROWS


def key_of(rows):
    return rows[0:1] * 65536.0 + rows[1:2] * 256.0 + rows[2:3]


def join_body(*refs):
    out, columns, start = refs[-1], [], 0
    for ref in refs[:-1]:
        size = count_of(ref) * ROWS
        out[start : start + size, :] = ref[0:size, :]
        width = -(-size // 128) * 128
        keys = ref[size : size + KEYS, 0:width].astype(jnp.float32)[0:8]
        columns.append(jnp.transpose(keys)[0:size])
        start += size
    rows = jnp.transpose(jnp.concatenate(columns, axis=0))
    out[start : start + KEYS, :] = jnp.zeros((KEYS, DIM), jnp.bfloat16)
    out[start : start + KEYS, 0:start] = jnp.concatenate([rows, jnp.zeros_like(rows)], axis=0).astype(jnp.bfloat16)


def join(name, *blocks, flops=0):
    total = sum(count_of(b) for b in blocks)
    shape = jax.ShapeDtypeStruct((total * ROWS + KEYS, DIM), jnp.bfloat16)
    return call(join_body, shape, count=len(blocks), flops=flops, name=name)(*blocks)


def highest(first, *rest):
    for rows in rest:
        first = jnp.maximum(first, rows)
    return first


def after_kernel(arrays, token):
    return lax.optimization_barrier((*arrays, token))[:-1]


def score(tasks, name, token=None, weight=1):
    arrays = []

    def place_of(array):
        for i, known in enumerate(arrays):
            if known is array:
                return i
        arrays.append(array)
        return len(arrays) - 1

    plan = [(place_of(query), count_of(query), [tuple(map(place_of, bundle)) for bundle in bundles]) for query, bundles in tasks]
    pairs = list(dict.fromkeys(pair for _, _, bundles in plan for pair in bundles))
    total, half = sum(count for _, count, _ in plan), 2 * ROWS

    def body(*args):
        refs, out, joined = args[: len(arrays)], args[-2], args[-1]
        parts = {}
        for i, (top, bottom) in enumerate(pairs):
            top, bottom = refs[top], refs[bottom]
            joined[i, 0:128, :] = top[256:half, :]
            joined[i, 128:256, :] = bottom[0:128, :]
            rows = [key_of(ref[half : half + KEYS, 0:half].astype(jnp.float32)[0:8]) for ref in (top, bottom)]
            key = jnp.concatenate(rows, axis=1)
            tiles = (lambda t=top: t[0:256, :], lambda i=i: joined[i], lambda b=bottom: b[128:half, :])
            parts[pairs[i]] = [(tile, key[:, 256 * j : 256 * j + 256]) for j, tile in enumerate(tiles)]
        row = 0
        for at, count, bundles in plan:
            q_ref, size = refs[at], count * ROWS
            width = -(-size // 128) * 128
            key_row = key_of(q_ref[size : size + KEYS, 0:width].astype(jnp.float32)[0:8])
            key_q = jnp.transpose(jnp.broadcast_to(key_row, (8, width)))[0:size, 0:1]
            base = jnp.floor(key_q * (1.0 / 65536.0)) * 65536.0
            best = jnp.full((size, 128), -1.0, jnp.float32)
            for bundle in bundles:
                for tile, key_k in parts[bundle]:
                    scores = lax.dot_general(
                        q_ref[0:size, :], tile(), (((1,), (1,)), ((), ())), preferred_element_type=jnp.float32
                    )
                    allowed = (key_k < key_q) & (key_k >= base)
                    scores = jnp.where(allowed, scores, -1.0)
                    best = jnp.maximum(best, jnp.maximum(scores[:, 0:128], scores[:, 128:256]))
            top = jnp.max(best, axis=1, keepdims=True)
            for i in range(count):
                out[row : row + 1, :] = column_to_row(top[i * ROWS : (i + 1) * ROWS])
                row += 1

    flops = sum(2 * DIM * ROWS * ROWS * count * 4 * len(bundles) for _, count, bundles in plan)
    operands = arrays if token is None else arrays + [token]
    return call(
        body,
        jax.ShapeDtypeStruct((total, ROWS), jnp.float32),
        scratch=[pltpu.VMEM((len(pairs), 256, DIM), jnp.bfloat16)],
        flops=int(flops * weight),
        count=len(operands),
        name=name,
    )(*operands)


def on_device(sketches, labels, ranks):
    core = lax.axis_index("core").astype(jnp.int32)
    z = lax.axis_index("z").astype(jnp.int32)
    place = jnp.stack([core, z])
    single = jax.ShapeDtypeStruct((ROWS + KEYS, DIM), jnp.bfloat16)
    own = call(normalise_body, single, spaces=[SMEM] + [VMEM] * 3, name="normalise")(
        place, sketches, labels.reshape(1, ROWS), ranks.reshape(1, ROWS)
    )

    def first(step):
        return lambda x, c, z, y: (x + step * (1 - c), c, z, y + step * c)

    def second(step):
        return lambda x, c, z, y: (x + step * c, c, z, y + step * (1 - c))

    def along_z(x, c, z, y):
        return (x, c, z + 1 - 2 * c, y)

    def across(x, c, z, y):
        return (x, c + 1, z, y)

    partner = send(own, across, "partner")
    key_far, key_up, key_down = send(own, first(2), "key_far"), send(own, first(1), "key_up"), send(own, first(-1), "key_down")
    here = join("here", own, partner, flops=4 << 30)
    r1 = send(here, along_z, "r1")
    ka = join("ka", own, key_down)
    after_a, before_a = send(ka, second(-1), "ka_down"), send(ka, second(1), "ka_up")
    key_far, key_up = after_kernel([key_far, key_up], ka)
    kb = join("kb", key_up, key_far)
    base = [(ka, kb)]
    s0 = score([(here, base)], "s0", weight=10)
    (r1,) = after_kernel([r1], s0)
    r2, e1 = send(r1, along_z, "r2"), send(r1, across, "e1")
    s1 = score([(r1, base)], "s1", weight=10)
    after_a, before_a, e1 = after_kernel([after_a, before_a, e1], s1)
    (kb_later,) = after_kernel([kb], before_a)
    after_b, before_b = send(kb_later, second(-1), "kb_down"), send(kb_later, second(1), "kb_up")
    opposite_a = send(before_a, second(1), "opposite_a")
    near_a = [(after_a, before_a)]
    s2 = score([(here, near_a), (r1, near_a), (e1, base + near_a)], "s2", weight=W2)
    (r2,) = after_kernel([r2], s2)
    r3, e2 = send(r2, along_z, "r3"), send(r2, across, "e2")
    s3 = score([(r2, base + near_a)], "s3", weight=W3)
    (e2,) = after_kernel([e2], s3)
    s4 = score([(e2, base + near_a)], "s4", weight=W3)
    after_b, before_b = after_kernel([after_b, before_b], s4)
    opposite_b = send(after_b, second(-1), "opposite_b")
    near_b = [(after_b, before_b)]
    s5 = score([(q, near_b) for q in (here, r1, e1, r2, e2)], "s5", weight=W5)
    (r3,) = after_kernel([r3], s5)
    r4, e3 = send(r3, along_z, "r4"), send(r3, across, "e3")
    s7 = score([(r3, base + near_a + near_b)], "s7", weight=W7)
    (e3,) = after_kernel([e3], s7)
    s6 = score([(e3, base + near_a + near_b)], "s6", weight=W6)
    opposite_a, opposite_b = after_kernel([opposite_a, opposite_b], s6)
    opposite = [(opposite_a, opposite_b)]
    s8 = score([(q, opposite) for q in (here, r1, e1, r2, e2, r3, e3)], "s8")
    (r4,) = after_kernel([r4], s8)
    s9 = score([(r4, base + near_a + near_b + opposite)], "s9")

    def merge_body(at, s0, s1, s2, s3, s4, s5, s6, s7, s8, s9, out):
        me, level = at[0], at[1]
        sign = 2 * me - 1
        two, five, eight = s2[...], s5[...], s8[...]
        groups = (
            (highest(s0[...], two[0:2], five[0:2], eight[0:2]), 0),
            (highest(s1[...], two[2:4], five[2:4], eight[2:4]), sign),
            (highest(two[4:6], five[4:6], eight[4:6]), -sign),
            (highest(s3[...], five[6:8], eight[6:8]), 2 * sign),
            (highest(s4[...], five[8:10], eight[8:10]), -2 * sign),
            (highest(s7[...], eight[10:12]), 3 * sign),
            (highest(s6[...], eight[12:14]), -3 * sign),
            (s9[...], 4),
        )
        for k, (rows, step) in enumerate(groups):
            for j in range(2):
                which = me if (j == 0) != (k in (2, 4, 6)) else 1 - me
                out[pl.ds(which * 8 + lax.rem(level + step + 16, 8), 1), :] = rows[j : j + 1]

    scores = (s0, s1, s2, s3, s4, s5, s6, s7, s8, s9)
    partial = call(
        merge_body, jax.ShapeDtypeStruct((16, ROWS), jnp.float32), spaces=[SMEM] + [VMEM] * len(scores), name="merge"
    )(place, *scores)
    returned = lax.all_to_all(partial, ("core", "z"), split_axis=0, concat_axis=0, tiled=True)
    return jnp.max(returned, axis=0)


def solution(mesh):
    fine = Mesh(mesh.devices.reshape(SIZES), AXES)
    return jax.shard_map(
        on_device,
        mesh=fine,
        in_specs=(P(AXES, None), P(AXES, None), P(AXES)),
        out_specs=P(AXES),
        check_vma=False,
    )
```

time: 87.9 us -> 86.2 us (0.981)
  waiting for transfers between devices: 16.3 us -> 6.4 us
  starting transfers between devices: 31.1 us -> 36 us
  blocking collectives: 10.8 us -> 14.4 us
  local copies, waits for them, and re-layouts: 2.73 us -> 1.84 us
    ppermute x15 -> x17, waiting for transfers between devices: 16.3 us -> 6.4 us  [send(): return lax.ppermute(array, AXES, permutation(move))]
    ppermute x15 -> x17, starting transfers between devices: 31.1 us -> 36 us  [send(): return lax.ppermute(array, AXES, permutation(move))]
    all_to_all x1, blocking collectives: 10.8 us -> 14.4 us  [on_device(): lax.all_to_all(partial, ('core', 'z'), split_axis=0, concat_axis=0, tiled...]
    unnamed x5 -> x6, local copies, waits for them, and re-layouts: 2.6 us -> 1.83 us
    pallas_call x7 -> x10, Pallas kernels: 23.9 us -> 24.6 us  [score(): call(body, jax.ShapeDtypeStruct((total, ROWS), jnp.float32), scratch=[plt...]
  transfers between devices with their start and end apart: 15 -> 17, of which waited for: 6 -> 4; matrix products, arithmetic and copies ran while one was open for 0% -> 0% of each run, Pallas kernels for 24% -> 26%
where the time goes in v3:
time: 86.2 us; the launch traced here: 85.9 us
  starting transfers between devices  36 us (42%)
  Pallas kernels  26.5 us (31%)
  blocking collectives  14.4 us (17%)
  waiting for transfers between devices  6.4 us (7%)
  local copies, waits for them, and re-layouts  1.84 us (2%)
    ppermute x17, starting transfers between devices, send(): return lax.ppermute(array, AXES, permutation(move))  36 us
    pallas_call x10, Pallas kernels, score(): call(body, jax.ShapeDtypeStruct((total, ROWS), jnp.float32), scratch=[plt...  24.6 us
    all_to_all x1, blocking collectives, on_device(): lax.all_to_all(partial, ('core', 'z'), split_axis=0, concat_axis=0, tiled...  14.4 us
    ppermute x17, waiting for transfers between devices, send(): return lax.ppermute(array, AXES, permutation(move))  6.4 us
    unnamed x6, local copies, waits for them, and re-layouts  1.83 us
  transfers between devices with their start and end apart: 17, of which 4 were waited for; matrix products, arithmetic and copies ran while one was open for 0% of the time, Pallas kernels for 26%

profile of v3, /device:TPU:1, one launch (start us, length us, event | category | flops | bytes accessed | tf_op | source)
XLA Modules:
  0.0 85.9 jit_solution(18276454057587203229)
XLA Ops:
  0.8 1.1 %copy-done = f32[192,1024]{1,0:T(8,128)S(1)} copy-done((f32[192,1024]{1,0:T(8,128)S(1)}, f32[192,1024]{1,0:T(8,128)}, u32[]{:S(2)}) %copy-start) | copy-done | bytes 786456
  2.6 3.3 %collective-permute-start = (bf16[208,1024]{1,0:T(8,128)(2,1)S(1)}, bf16[208,1024]{1,0:T(8,128)(2,1)S(1)}, u32[]{:S(2)}, u32[]{:S(2)}) collective-permute-start(bf16[208,1024]{1,0:T(8,128)(2,1)S(1)} %normalise.1.refs_0_), channel_id=1, source_target_pairs={{0,32},{1,33},{2,34},{3,35},{4,36},{5,37},{6,38},{7,39},{8,40},{9,... | collective-permute-start | bytes 1277960 | tf_op jit(solution)/shard_map/partner/ppermute | solution.py:30
  5.9 1.0 %collective-permute-start.1 = (bf16[208,1024]{1,0:T(8,128)(2,1)S(1)}, bf16[208,1024]{1,0:T(8,128)(2,1)S(1)}, u32[]{:S(2)}, u32[]{:S(2)}) collective-permute-start(bf16[208,1024]{1,0:T(8,128)(2,1)S(1)} %normalise.1.refs_0_), channel_id=1, source_target_pairs={{0,192},{1,193},{2,194},{3,195},{4,196},{5,197},{6,198},{7,199},{8... | collective-permute-start | bytes 1277960 | tf_op jit(solution)/shard_map/key_down/ppermute | solution.py:30
  8.2 5.6 %collective-permute-start.4 = (bf16[400,1024]{1,0:T(8,128)(2,1)S(1)}, bf16[400,1024]{1,0:T(8,128)(2,1)S(1)}, u32[]{:S(2)}, u32[]{:S(2)}) collective-permute-start(bf16[400,1024]{1,0:T(8,128)(2,1)S(1)} %here.1.args_0_), channel_id=1, source_target_pairs={{0,4},{1,5},{2,6},{3,7},{4,8},{5,9},{6,10},{7,11},{8,12},{9,13},{1... | collective-permute-start | bytes 2457608 | tf_op jit(solution)/shard_map/r1/ppermute | solution.py:30
  14.0 5.3 %collective-permute-start.5 = (bf16[400,1024]{1,0:T(8,128)(2,1)S(1)}, bf16[400,1024]{1,0:T(8,128)(2,1)S(1)}, u32[]{:S(2)}, u32[]{:S(2)}) collective-permute-start(bf16[400,1024]{1,0:T(8,128)(2,1)S(1)} %ka.1.args_1_.args_5_), channel_id=1, source_target_pairs={{0,3},{1,0},{2,1},{3,2},{4,7},{5,4},{6,5},{7,6},{8,11},{9,8},{10,9... | collective-permute-start | bytes 2457608 | tf_op jit(solution)/shard_map/ka_down/ppermute | solution.py:30
  20.5 1.0 %s0.1 = f32[2,192]{1,0:T(2,128)S(1)} custom-call(bf16[400,1024]{1,0:T(8,128)(2,1)S(1)} %here.1.args_0_, bf16[400,1024]{1,0:T(8,128)(2,1)S(1)} %ka.1.args_1_.args_5_, bf16[400,1024]{1,0:T(8,128)(2,1)S(1)} %kb.1.args_2_.args_6_), custom_call_target="tpu_custom_call" | custom-call | flops 6039797760 | tf_op jit(solution)/shard_map/s0/pallas_call | solution.py:151
  21.5 1.6 %collective-permute-done.4.args_0_.args_3_ = bf16[400,1024]{1,0:T(8,128)(2,1)S(1)} collective-permute-done((bf16[400,1024]{1,0:T(8,128)(2,1)S(1)}, bf16[400,1024]{1,0:T(8,128)(2,1)S(1)}, u32[]{:S(2)}, u32[]{:S(2)}) %collective-permute-start.4) | collective-permute-done | bytes 819232 | tf_op jit(solution)/shard_map/r1/ppermute | solution.py:30
  23.1 2.1 %collective-permute-start.7 = (bf16[400,1024]{1,0:T(8,128)(2,1)S(1)}, bf16[400,1024]{1,0:T(8,128)(2,1)S(1)}, u32[]{:S(2)}, u32[]{:S(2)}) collective-permute-start(bf16[400,1024]{1,0:T(8,128)(2,1)S(1)} %collective-permute-done.4.args_0_.args_3_), channel_id=1, source_target_pairs={{0,32},{1,33},{2,34},{3,35},{4,36},{5,37},{6,38},{7,39},{8,40},{9,... | collective-permute-start | bytes 2457608 | tf_op jit(solution)/shard_map/e1/ppermute | solution.py:30
  25.2 3.0 %collective-permute-start.8 = (bf16[400,1024]{1,0:T(8,128)(2,1)S(1)}, bf16[400,1024]{1,0:T(8,128)(2,1)S(1)}, u32[]{:S(2)}, u32[]{:S(2)}) collective-permute-start(bf16[400,1024]{1,0:T(8,128)(2,1)S(1)} %collective-permute-done.4.args_0_.args_3_), channel_id=1, source_target_pairs={{0,4},{1,5},{2,6},{3,7},{4,8},{5,9},{6,10},{7,11},{8,12},{9,13},{1... | collective-permute-start | bytes 2457608 | tf_op jit(solution)/shard_map/r2/ppermute | solution.py:30
  29.1 2.9 %collective-permute-done.6.args_2_.args_4_ = bf16[400,1024]{1,0:T(8,128)(2,1)S(1)} collective-permute-done((bf16[400,1024]{1,0:T(8,128)(2,1)S(1)}, bf16[400,1024]{1,0:T(8,128)(2,1)S(1)}, u32[]{:S(2)}, u32[]{:S(2)}) %collective-permute-start.6) | collective-permute-done | bytes 819232 | tf_op jit(solution)/shard_map/ka_up/ppermute | solution.py:30
  32.0 1.5 %collective-permute-start.11 = (bf16[400,1024]{1,0:T(8,128)(2,1)S(1)}, bf16[400,1024]{1,0:T(8,128)(2,1)S(1)}, u32[]{:S(2)}, u32[]{:S(2)}) collective-permute-start(bf16[400,1024]{1,0:T(8,128)(2,1)S(1)} %kb.1.args_2_.args_6_), channel_id=1, source_target_pairs={{0,1},{1,2},{2,3},{3,0},{4,5},{5,6},{6,7},{7,4},{8,9},{9,10},{10,1... | collective-permute-start | bytes 2457608 | tf_op jit(solution)/shard_map/kb_up/ppermute | solution.py:30
  33.5 3.0 %s2_.1.s2 = f32[6,192]{1,0:T(8,128)S(1)} custom-call(bf16[400,1024]{1,0:T(8,128)(2,1)S(1)} %here.1.args_0_, bf16[400,1024]{1,0:T(8,128)(2,1)S(1)} %collective-permute-done.5.args_1_.args_3_, bf16[400,1024]{1,0:T(8,128)(2,1)S(1)} %collective-permute-done.6.args_2_.args_4_, bf16[400,1024]{1,0:T(8,128)(2,1)S(1)} %collective-permute-done.4.args_0_.args_3_, ...), custom_call_target="tpu_custom_call" | custom-call | flops 24159191040 | tf_op jit(solution)/shard_map/s2/pallas_call | solution.py:151
  37.4 1.8 %collective-permute-start.9 = (bf16[400,1024]{1,0:T(8,128)(2,1)S(1)}, bf16[400,1024]{1,0:T(8,128)(2,1)S(1)}, u32[]{:S(2)}, u32[]{:S(2)}) collective-permute-start(bf16[400,1024]{1,0:T(8,128)(2,1)S(1)} %collective-permute-done.8.args_0_.args_5_), channel_id=1, source_target_pairs={{0,32},{1,33},{2,34},{3,35},{4,36},{5,37},{6,38},{7,39},{8,40},{9,... | collective-permute-start | bytes 2457608 | tf_op jit(solution)/shard_map/e2/ppermute | solution.py:30
  39.3 5.6 %collective-permute-start.12 = (bf16[400,1024]{1,0:T(8,128)(2,1)S(1)}, bf16[400,1024]{1,0:T(8,128)(2,1)S(1)}, u32[]{:S(2)}, u32[]{:S(2)}) collective-permute-start(bf16[400,1024]{1,0:T(8,128)(2,1)S(1)} %collective-permute-done.8.args_0_.args_5_), channel_id=1, source_target_pairs={{0,4},{1,5},{2,6},{3,7},{4,8},{5,9},{6,10},{7,11},{8,12},{9,13},{1... | collective-permute-start | bytes 2457608 | tf_op jit(solution)/shard_map/r3/ppermute | solution.py:30
  44.8 1.6 %s3.1 = f32[2,192]{1,0:T(2,128)S(1)} custom-call(bf16[400,1024]{1,0:T(8,128)(2,1)S(1)} %collective-permute-done.8.args_0_.args_5_, bf16[400,1024]{1,0:T(8,128)(2,1)S(1)} %ka.1.args_1_.args_5_, bf16[400,1024]{1,0:T(8,128)(2,1)S(1)} %kb.1.args_2_.args_6_, bf16[400,1024]{1,0:T(8,128)(2,1)S(1)} %collective-permute-done.5.args_1_.args_3_, ...), custom_call_target="tpu_custom_call" | custom-call | flops 12079595520 | tf_op jit(solution)/shard_map/s3/pallas_call | solution.py:151
  46.4 1.6 %s4_.1.s4 = f32[2,192]{1,0:T(2,128)S(1)} custom-call(bf16[400,1024]{1,0:T(8,128)(2,1)S(1)} %collective-permute-done.9.args_0_.args_6_, bf16[400,1024]{1,0:T(8,128)(2,1)S(1)} %ka.1.args_1_.args_5_, bf16[400,1024]{1,0:T(8,128)(2,1)S(1)} %kb.1.args_2_.args_6_, bf16[400,1024]{1,0:T(8,128)(2,1)S(1)} %collective-permute-done.5.args_1_.args_3_, ...), custom_call_target="tpu_custom_call" | custom-call | flops 12079595520 | tf_op jit(solution)/shard_map/s4/pallas_call | solution.py:151
  48.1 3.5 %collective-permute-start.15 = (bf16[400,1024]{1,0:T(8,128)(2,1)S(1)}, bf16[400,1024]{1,0:T(8,128)(2,1)S(1)}, u32[]{:S(2)}, u32[]{:S(2)}) collective-permute-start(bf16[400,1024]{1,0:T(8,128)(2,1)S(1)} %collective-permute-done.10.args_1_.args_5_), channel_id=1, source_target_pairs={{0,3},{1,0},{2,1},{3,2},{4,7},{5,4},{6,5},{7,6},{8,11},{9,8},{10,9... | collective-permute-start | bytes 2457608 | tf_op jit(solution)/shard_map/opposite_b/ppermute | solution.py:30
  51.5 3.7 %s5.1 = f32[10,192]{1,0:T(8,128)S(1)} custom-call(bf16[400,1024]{1,0:T(8,128)(2,1)S(1)} %here.1.args_0_, bf16[400,1024]{1,0:T(8,128)(2,1)S(1)} %collective-permute-done.10.args_1_.args_5_, bf16[400,1024]{1,0:T(8,128)(2,1)S(1)} %collective-permute-done.11.args_2_.args_6_, bf16[400,1024]{1,0:T(8,128)(2,1)S(1)} %collective-permute-done.4.args_0_.args_3_, ...), custom_call_target="tpu_custom_call" | custom-call | flops 3019898880 | tf_op jit(solution)/shard_map/s5/pallas_call | solution.py:151
  55.5 2.0 %collective-permute-start.16 = (bf16[400,1024]{1,0:T(8,128)(2,1)S(1)}, bf16[400,1024]{1,0:T(8,128)(2,1)S(1)}, u32[]{:S(2)}, u32[]{:S(2)}) collective-permute-start(bf16[400,1024]{1,0:T(8,128)(2,1)S(1)} %collective-permute-done.12.args_0_.args_7_), channel_id=1, source_target_pairs={{0,4},{1,5},{2,6},{3,7},{4,8},{5,9},{6,10},{7,11},{8,12},{9,13},{1... | collective-permute-start | bytes 2457608 | tf_op jit(solution)/shard_map/r4/ppermute | solution.py:30
  57.5 2.3 %s7.1 = f32[2,192]{1,0:T(2,128)S(1)} custom-call(bf16[400,1024]{1,0:T(8,128)(2,1)S(1)} %collective-permute-done.12.args_0_.args_7_, bf16[400,1024]{1,0:T(8,128)(2,1)S(1)} %ka.1.args_1_.args_5_, bf16[400,1024]{1,0:T(8,128)(2,1)S(1)} %kb.1.args_2_.args_6_, bf16[400,1024]{1,0:T(8,128)(2,1)S(1)} %collective-permute-done.5.args_1_.args_3_, ...), custom_call_target="tpu_custom_call" | custom-call | flops 18119393280 | tf_op jit(solution)/shard_map/s7/pallas_call | solution.py:151
  59.9 2.3 %s6.1 = f32[2,192]{1,0:T(2,128)S(1)} custom-call(bf16[400,1024]{1,0:T(8,128)(2,1)S(1)} %collective-permute-done.13.args_0_.args_8_, bf16[400,1024]{1,0:T(8,128)(2,1)S(1)} %ka.1.args_1_.args_5_, bf16[400,1024]{1,0:T(8,128)(2,1)S(1)} %kb.1.args_2_.args_6_, bf16[400,1024]{1,0:T(8,128)(2,1)S(1)} %collective-permute-done.5.args_1_.args_3_, ...), custom_call_target="tpu_custom_call" | custom-call | flops 1811939328 | tf_op jit(solution)/shard_map/s6/pallas_call | solution.py:151
  62.2 5.1 %s8_.1.s8 = f32[14,192]{1,0:T(8,128)S(1)} custom-call(bf16[400,1024]{1,0:T(8,128)(2,1)S(1)} %here.1.args_0_, bf16[400,1024]{1,0:T(8,128)(2,1)S(1)} %collective-permute-done.14.args_1_.args_7_, bf16[400,1024]{1,0:T(8,128)(2,1)S(1)} %collective-permute-done.15.args_2_.args_8_, bf16[400,1024]{1,0:T(8,128)(2,1)S(1)} %collective-permute-done.4.args_0_.args_3_, ...), custom_call_target="tpu_custom_call" | custom-call | flops 4227858432 | tf_op jit(solution)/shard_map/s8/pallas_call | solution.py:151
  67.3 3.0 %s9.1 = f32[2,192]{1,0:T(2,128)S(1)} custom-call(bf16[400,1024]{1,0:T(8,128)(2,1)S(1)} %collective-permute-done.16.args_0_, bf16[400,1024]{1,0:T(8,128)(2,1)S(1)} %ka.1.args_1_.args_5_, bf16[400,1024]{1,0:T(8,128)(2,1)S(1)} %kb.1.args_2_.args_6_, bf16[400,1024]{1,0:T(8,128)(2,1)S(1)} %collective-permute-done.5.args_1_.args_3_, ...), custom_call_target="tpu_custom_call" | custom-call | flops 2415919104 | tf_op jit(solution)/shard_map/s9/pallas_call | solution.py:151
  70.9 14.4 %all_to_all.9 = f32[16,1,192]{2,1,0:T(1,128)S(1)} all-to-all(f32[16,1,192]{2,1,0:T(1,128)S(1)} %copy.4), channel_id=1, replica_groups=mesh['x'=4,'core'=2,'z'=8,'y'=4] {'core','z'}, dimensions={0} | all-to-all | bytes 24576 | tf_op jit(solution)/shard_map/all_to_all | solution.py:244
  (35 shorter events, 7.5 us)
Async XLA Ops:
  0.1 0.7 copy-start.2
  0.1 0.7 copy-start.1
  0.8 1.1 %copy-start = (f32[192,1024]{1,0:T(8,128)S(1)}, f32[192,1024]{1,0:T(8,128)}, u32[]{:S(2)}) copy-start(f32[192,1024]{1,0:T(8,128)} %sketches.1) | copy-start | bytes 2359300
  2.6 5.4 %collective-permute-start = (bf16[208,1024]{1,0:T(8,128)(2,1)S(1)}, bf16[208,1024]{1,0:T(8,128)(2,1)S(1)}, u32[]{:S(2)}, u32[]{:S(2)}) collective-permute-start(bf16[208,1024]{1,0:T(8,128)(2,1)S(1)} %normalise.1.refs_0_), channel_id=1, source_target_pairs={{0,32},{1,33},{2,34},{3,35},{4,36},{5,37},{6,38},{7,39},{8,40},{9,... | collective-permute-start | bytes 1277960 | tf_op jit(solution)/shard_map/partner/ppermute | solution.py:30
  5.9 7.9 %collective-permute-start.1 = (bf16[208,1024]{1,0:T(8,128)(2,1)S(1)}, bf16[208,1024]{1,0:T(8,128)(2,1)S(1)}, u32[]{:S(2)}, u32[]{:S(2)}) collective-permute-start(bf16[208,1024]{1,0:T(8,128)(2,1)S(1)} %normalise.1.refs_0_), channel_id=1, source_target_pairs={{0,192},{1,193},{2,194},{3,195},{4,196},{5,197},{6,198},{7,199},{8... | collective-permute-start | bytes 1277960 | tf_op jit(solution)/shard_map/key_down/ppermute | solution.py:30
  6.9 12.4 %collective-permute-start.2 = (bf16[208,1024]{1,0:T(8,128)(2,1)S(1)}, bf16[208,1024]{1,0:T(8,128)(2,1)S(1)}, u32[]{:S(2)}, u32[]{:S(2)}) collective-permute-start(bf16[208,1024]{1,0:T(8,128)(2,1)S(1)} %normalise.1.refs_0_), channel_id=1, source_target_pairs={{0,128},{1,129},{2,130},{3,131},{4,132},{5,133},{6,134},{7,135},{8... | collective-permute-start | bytes 1277960 | tf_op jit(solution)/shard_map/key_far/ppermute | solution.py:30
  7.3 13.0 %collective-permute-start.3 = (bf16[208,1024]{1,0:T(8,128)(2,1)S(1)}, bf16[208,1024]{1,0:T(8,128)(2,1)S(1)}, u32[]{:S(2)}, u32[]{:S(2)}) collective-permute-start(bf16[208,1024]{1,0:T(8,128)(2,1)S(1)} %normalise.1.refs_0_), channel_id=1, source_target_pairs={{0,64},{1,65},{2,66},{3,67},{4,68},{5,69},{6,70},{7,71},{8,72},{9,... | collective-permute-start | bytes 1277960 | tf_op jit(solution)/shard_map/key_up/ppermute | solution.py:30
  8.2 14.9 %collective-permute-start.4 = (bf16[400,1024]{1,0:T(8,128)(2,1)S(1)}, bf16[400,1024]{1,0:T(8,128)(2,1)S(1)}, u32[]{:S(2)}, u32[]{:S(2)}) collective-permute-start(bf16[400,1024]{1,0:T(8,128)(2,1)S(1)} %here.1.args_0_), channel_id=1, source_target_pairs={{0,4},{1,5},{2,6},{3,7},{4,8},{5,9},{6,10},{7,11},{8,12},{9,13},{1... | collective-permute-start | bytes 2457608 | tf_op jit(solution)/shard_map/r1/ppermute | solution.py:30
  14.0 15.1 %collective-permute-start.5 = (bf16[400,1024]{1,0:T(8,128)(2,1)S(1)}, bf16[400,1024]{1,0:T(8,128)(2,1)S(1)}, u32[]{:S(2)}, u32[]{:S(2)}) collective-permute-start(bf16[400,1024]{1,0:T(8,128)(2,1)S(1)} %ka.1.args_1_.args_5_), channel_id=1, source_target_pairs={{0,3},{1,0},{2,1},{3,2},{4,7},{5,4},{6,5},{7,6},{8,11},{9,8},{10,9... | collective-permute-start | bytes 2457608 | tf_op jit(solution)/shard_map/ka_down/ppermute | solution.py:30
  19.3 12.7 %collective-permute-start.6 = (bf16[400,1024]{1,0:T(8,128)(2,1)S(1)}, bf16[400,1024]{1,0:T(8,128)(2,1)S(1)}, u32[]{:S(2)}, u32[]{:S(2)}) collective-permute-start(bf16[400,1024]{1,0:T(8,128)(2,1)S(1)} %ka.1.args_1_.args_5_), channel_id=1, source_target_pairs={{0,1},{1,2},{2,3},{3,0},{4,5},{5,6},{6,7},{7,4},{8,9},{9,10},{10,1... | collective-permute-start | bytes 2457608 | tf_op jit(solution)/shard_map/ka_up/ppermute | solution.py:30
  23.1 8.9 %collective-permute-start.7 = (bf16[400,1024]{1,0:T(8,128)(2,1)S(1)}, bf16[400,1024]{1,0:T(8,128)(2,1)S(1)}, u32[]{:S(2)}, u32[]{:S(2)}) collective-permute-start(bf16[400,1024]{1,0:T(8,128)(2,1)S(1)} %collective-permute-done.4.args_0_.args_3_), channel_id=1, source_target_pairs={{0,32},{1,33},{2,34},{3,35},{4,36},{5,37},{6,38},{7,39},{8,40},{9,... | collective-permute-start | bytes 2457608 | tf_op jit(solution)/shard_map/e1/ppermute | solution.py:30
  25.2 12.2 %collective-permute-start.8 = (bf16[400,1024]{1,0:T(8,128)(2,1)S(1)}, bf16[400,1024]{1,0:T(8,128)(2,1)S(1)}, u32[]{:S(2)}, u32[]{:S(2)}) collective-permute-start(bf16[400,1024]{1,0:T(8,128)(2,1)S(1)} %collective-permute-done.4.args_0_.args_3_), channel_id=1, source_target_pairs={{0,4},{1,5},{2,6},{3,7},{4,8},{5,9},{6,10},{7,11},{8,12},{9,13},{1... | collective-permute-start | bytes 2457608 | tf_op jit(solution)/shard_map/r2/ppermute | solution.py:30
  32.0 16.1 %collective-permute-start.10 = (bf16[400,1024]{1,0:T(8,128)(2,1)S(1)}, bf16[400,1024]{1,0:T(8,128)(2,1)S(1)}, u32[]{:S(2)}, u32[]{:S(2)}) collective-permute-start(bf16[400,1024]{1,0:T(8,128)(2,1)S(1)} %kb.1.args_2_.args_6_), channel_id=1, source_target_pairs={{0,3},{1,0},{2,1},{3,2},{4,7},{5,4},{6,5},{7,6},{8,11},{9,8},{10,9... | collective-permute-start | bytes 2457608 | tf_op jit(solution)/shard_map/kb_down/ppermute | solution.py:30
  32.0 16.1 %collective-permute-start.11 = (bf16[400,1024]{1,0:T(8,128)(2,1)S(1)}, bf16[400,1024]{1,0:T(8,128)(2,1)S(1)}, u32[]{:S(2)}, u32[]{:S(2)}) collective-permute-start(bf16[400,1024]{1,0:T(8,128)(2,1)S(1)} %kb.1.args_2_.args_6_), channel_id=1, source_target_pairs={{0,1},{1,2},{2,3},{3,0},{4,5},{5,6},{6,7},{7,4},{8,9},{9,10},{10,1... | collective-permute-start | bytes 2457608 | tf_op jit(solution)/shard_map/kb_up/ppermute | solution.py:30
  37.4 9.0 %collective-permute-start.9 = (bf16[400,1024]{1,0:T(8,128)(2,1)S(1)}, bf16[400,1024]{1,0:T(8,128)(2,1)S(1)}, u32[]{:S(2)}, u32[]{:S(2)}) collective-permute-start(bf16[400,1024]{1,0:T(8,128)(2,1)S(1)} %collective-permute-done.8.args_0_.args_5_), channel_id=1, source_target_pairs={{0,32},{1,33},{2,34},{3,35},{4,36},{5,37},{6,38},{7,39},{8,40},{9,... | collective-permute-start | bytes 2457608 | tf_op jit(solution)/shard_map/e2/ppermute | solution.py:30
  39.3 15.9 %collective-permute-start.12 = (bf16[400,1024]{1,0:T(8,128)(2,1)S(1)}, bf16[400,1024]{1,0:T(8,128)(2,1)S(1)}, u32[]{:S(2)}, u32[]{:S(2)}) collective-permute-start(bf16[400,1024]{1,0:T(8,128)(2,1)S(1)} %collective-permute-done.8.args_0_.args_5_), channel_id=1, source_target_pairs={{0,4},{1,5},{2,6},{3,7},{4,8},{5,9},{6,10},{7,11},{8,12},{9,13},{1... | collective-permute-start | bytes 2457608 | tf_op jit(solution)/shard_map/r3/ppermute | solution.py:30
  44.8 17.4 %collective-permute-start.14 = (bf16[400,1024]{1,0:T(8,128)(2,1)S(1)}, bf16[400,1024]{1,0:T(8,128)(2,1)S(1)}, u32[]{:S(2)}, u32[]{:S(2)}) collective-permute-start(bf16[400,1024]{1,0:T(8,128)(2,1)S(1)} %collective-permute-done.6.args_2_.args_4_), channel_id=1, source_target_pairs={{0,1},{1,2},{2,3},{3,0},{4,5},{5,6},{6,7},{7,4},{8,9},{9,10},{10,1... | collective-permute-start | bytes 2457608 | tf_op jit(solution)/shard_map/opposite_a/ppermute | solution.py:30
  48.1 14.2 %collective-permute-start.15 = (bf16[400,1024]{1,0:T(8,128)(2,1)S(1)}, bf16[400,1024]{1,0:T(8,128)(2,1)S(1)}, u32[]{:S(2)}, u32[]{:S(2)}) collective-permute-start(bf16[400,1024]{1,0:T(8,128)(2,1)S(1)} %collective-permute-done.10.args_1_.args_5_), channel_id=1, source_target_pairs={{0,3},{1,0},{2,1},{3,2},{4,7},{5,4},{6,5},{7,6},{8,11},{9,8},{10,9... | collective-permute-start | bytes 2457608 | tf_op jit(solution)/shard_map/opposite_b/ppermute | solution.py:30
  55.2 4.7 %collective-permute-start.13 = (bf16[400,1024]{1,0:T(8,128)(2,1)S(1)}, bf16[400,1024]{1,0:T(8,128)(2,1)S(1)}, u32[]{:S(2)}, u32[]{:S(2)}) collective-permute-start(bf16[400,1024]{1,0:T(8,128)(2,1)S(1)} %collective-permute-done.12.args_0_.args_7_), channel_id=1, source_target_pairs={{0,32},{1,33},{2,34},{3,35},{4,36},{5,37},{6,38},{7,39},{8,40},{9,... | collective-permute-start | bytes 2457608 | tf_op jit(solution)/shard_map/e3/ppermute | solution.py:30
  55.5 11.8 %collective-permute-start.16 = (bf16[400,1024]{1,0:T(8,128)(2,1)S(1)}, bf16[400,1024]{1,0:T(8,128)(2,1)S(1)}, u32[]{:S(2)}, u32[]{:S(2)}) collective-permute-start(bf16[400,1024]{1,0:T(8,128)(2,1)S(1)} %collective-permute-done.12.args_0_.args_7_), channel_id=1, source_target_pairs={{0,4},{1,5},{2,6},{3,7},{4,8},{5,9},{6,10},{7,11},{8,12},{9,13},{1... | collective-permute-start | bytes 2457608 | tf_op jit(solution)/shard_map/r4/ppermute | solution.py:30

commit v4 on v3

--- a/solution.py
+++ b/solution.py
@@ -14,7 +14,6 @@
 KEYS = 16
 DIM = 1024
 VMEM = pl.BlockSpec(memory_space=pltpu.VMEM)
-SMEM = pl.BlockSpec(memory_space=pltpu.SMEM)
 
 
 def permutation(move):
@@ -49,7 +48,7 @@
     return jnp.sum(jnp.where(diagonal, column, 0.0), axis=0, keepdims=True)
 
 
-def normalise_body(_, sketches, labels, ranks, out):
+def normalise_body(sketches, labels, ranks, out):
     rank_row = ranks[...]
     high = (rank_row // 256).astype(jnp.float32)
     low = (rank_row % 256).astype(jnp.float32)
@@ -100,7 +99,7 @@
     return lax.optimization_barrier((*arrays, token))[:-1]
 
 
-def score(tasks, name, token=None, weight=1):
+def score(tasks, name, token=None, weight=1, extra=(), finish=None):
     arrays = []
 
     def place_of(array):
@@ -116,6 +115,7 @@
 
     def body(*args):
         refs, out, joined = args[: len(arrays)], args[-2], args[-1]
+        found = []
         parts = {}
         for i, (top, bottom) in enumerate(pairs):
             top, bottom = refs[top], refs[bottom]
@@ -125,7 +125,6 @@
             key = jnp.concatenate(rows, axis=1)
             tiles = (lambda t=top: t[0:256, :], lambda i=i: joined[i], lambda b=bottom: b[128:half, :])
             parts[pairs[i]] = [(tile, key[:, 256 * j : 256 * j + 256]) for j, tile in enumerate(tiles)]
-        row = 0
         for at, count, bundles in plan:
             q_ref, size = refs[at], count * ROWS
             width = -(-size // 128) * 128
@@ -143,14 +142,18 @@
                     best = jnp.maximum(best, jnp.maximum(scores[:, 0:128], scores[:, 128:256]))
             top = jnp.max(best, axis=1, keepdims=True)
             for i in range(count):
-                out[row : row + 1, :] = column_to_row(top[i * ROWS : (i + 1) * ROWS])
-                row += 1
+                found.append(column_to_row(top[i * ROWS : (i + 1) * ROWS]))
+        if finish is None:
+            for i, rows in enumerate(found):
+                out[i : i + 1, :] = rows
+        else:
+            finish(*args[len(arrays) : len(arrays) + len(extra)], jnp.concatenate(found, axis=0), out)
 
     flops = sum(2 * DIM * ROWS * ROWS * count * 4 * len(bundles) for _, count, bundles in plan)
-    operands = arrays if token is None else arrays + [token]
+    operands = arrays + list(extra) + ([] if token is None else [token])
     return call(
         body,
-        jax.ShapeDtypeStruct((total, ROWS), jnp.float32),
+        jax.ShapeDtypeStruct((total if finish is None else 16, ROWS), jnp.float32),
         scratch=[pltpu.VMEM((len(pairs), 256, DIM), jnp.bfloat16)],
         flops=int(flops * weight),
         count=len(operands),
@@ -159,12 +162,9 @@
 
 
 def on_device(sketches, labels, ranks):
-    core = lax.axis_index("core").astype(jnp.int32)
-    z = lax.axis_index("z").astype(jnp.int32)
-    place = jnp.stack([core, z])
     single = jax.ShapeDtypeStruct((ROWS + KEYS, DIM), jnp.bfloat16)
-    own = call(normalise_body, single, spaces=[SMEM] + [VMEM] * 3, name="normalise")(
-        place, sketches, labels.reshape(1, ROWS), ranks.reshape(1, ROWS)
+    own = call(normalise_body, single, count=3, name="normalise")(
+        sketches, labels.reshape(1, ROWS), ranks.reshape(1, ROWS)
     )
 
     def first(step):
@@ -216,10 +216,8 @@
     opposite = [(opposite_a, opposite_b)]
     s8 = score([(q, opposite) for q in (here, r1, e1, r2, e2, r3, e3)], "s8")
     (r4,) = after_kernel([r4], s8)
-    s9 = score([(r4, base + near_a + near_b + opposite)], "s9")
-
-    def merge_body(at, s0, s1, s2, s3, s4, s5, s6, s7, s8, s9, out):
-        me, level = at[0], at[1]
+    def merge_body(s0, s1, s2, s3, s4, s5, s6, s7, s8, s9, out):
+        me, level = lax.axis_index("core"), lax.axis_index("z")
         sign = 2 * me - 1
         two, five, eight = s2[...], s5[...], s8[...]
         groups = (
@@ -230,17 +228,15 @@
             (highest(s4[...], five[8:10], eight[8:10]), -2 * sign),
             (highest(s7[...], eight[10:12]), 3 * sign),
             (highest(s6[...], eight[12:14]), -3 * sign),
-            (s9[...], 4),
+            (s9, 4),
         )
         for k, (rows, step) in enumerate(groups):
             for j in range(2):
                 which = me if (j == 0) != (k in (2, 4, 6)) else 1 - me
                 out[pl.ds(which * 8 + lax.rem(level + step + 16, 8), 1), :] = rows[j : j + 1]
 
-    scores = (s0, s1, s2, s3, s4, s5, s6, s7, s8, s9)
-    partial = call(
-        merge_body, jax.ShapeDtypeStruct((16, ROWS), jnp.float32), spaces=[SMEM] + [VMEM] * len(scores), name="merge"
-    )(place, *scores)
+    scores = (s0, s1, s2, s3, s4, s5, s6, s7, s8)
+    partial = score([(r4, base + near_a + near_b + opposite)], "s9", extra=scores, finish=merge_body)
     returned = lax.all_to_all(partial, ("core", "z"), split_axis=0, concat_axis=0, tiled=True)
     return jnp.max(returned, axis=0)
 

time: 86.2 us -> 85 us (0.986)
  Pallas kernels: 26.5 us -> 25.1 us
    pallas_call x12 -> x11, Pallas kernels: 25.8 us -> 24.5 us  [the longest x10 24.4 us: score(): call(body, jax.ShapeDtypeStruct((total if finish is None else 16, ROWS),...]
where the time goes in v4:
time: 85 us; the launch traced here: 84.7 us
  starting transfers between devices  36 us (42%)
  Pallas kernels  25.1 us (30%)
  blocking collectives  14.5 us (17%)
  waiting for transfers between devices  6.43 us (8%)
  local copies, waits for them, and re-layouts  1.84 us (2%)
    ppermute x17, starting transfers between devices, send(): return lax.ppermute(array, AXES, permutation(move))  36 us
    pallas_call x10, Pallas kernels, score(): call(body, jax.ShapeDtypeStruct((total if finish is None else 16, ROWS),...  24.4 us
    all_to_all x1, blocking collectives, on_device(): lax.all_to_all(partial, ('core', 'z'), split_axis=0, concat_axis=0, tiled...  14.5 us
    ppermute x17, waiting for transfers between devices, send(): return lax.ppermute(array, AXES, permutation(move))  6.43 us
    unnamed x6, local copies, waits for them, and re-layouts  1.83 us
  transfers between devices with their start and end apart: 17, of which 4 were waited for; matrix products, arithmetic and copies ran while one was open for 0% of the time, Pallas kernels for 26%

profile of v4, /device:TPU:1, one launch (start us, length us, event | category | flops | bytes accessed | tf_op | source)
XLA Modules:
  0.0 84.7 jit_solution(13231051239422864519)
XLA Ops:
  0.7 1.1 %copy-done = f32[192,1024]{1,0:T(8,128)S(1)} copy-done((f32[192,1024]{1,0:T(8,128)S(1)}, f32[192,1024]{1,0:T(8,128)}, u32[]{:S(2)}) %copy-start) | copy-done | bytes 786456
  2.0 3.3 %collective-permute-start = (bf16[208,1024]{1,0:T(8,128)(2,1)S(1)}, bf16[208,1024]{1,0:T(8,128)(2,1)S(1)}, u32[]{:S(2)}, u32[]{:S(2)}) collective-permute-start(bf16[208,1024]{1,0:T(8,128)(2,1)S(1)} %normalise.1.refs_0_), channel_id=1, source_target_pairs={{0,32},{1,33},{2,34},{3,35},{4,36},{5,37},{6,38},{7,39},{8,40},{9,... | collective-permute-start | bytes 1277960 | tf_op jit(solution)/shard_map/partner/ppermute | solution.py:29
  5.3 1.0 %collective-permute-start.2 = (bf16[208,1024]{1,0:T(8,128)(2,1)S(1)}, bf16[208,1024]{1,0:T(8,128)(2,1)S(1)}, u32[]{:S(2)}, u32[]{:S(2)}) collective-permute-start(bf16[208,1024]{1,0:T(8,128)(2,1)S(1)} %normalise.1.refs_0_), channel_id=1, source_target_pairs={{0,192},{1,193},{2,194},{3,195},{4,196},{5,197},{6,198},{7,199},{8... | collective-permute-start | bytes 1277960 | tf_op jit(solution)/shard_map/key_down/ppermute | solution.py:29
  7.6 5.6 %collective-permute-start.1 = (bf16[400,1024]{1,0:T(8,128)(2,1)S(1)}, bf16[400,1024]{1,0:T(8,128)(2,1)S(1)}, u32[]{:S(2)}, u32[]{:S(2)}) collective-permute-start(bf16[400,1024]{1,0:T(8,128)(2,1)S(1)} %here.1.args_0_), channel_id=1, source_target_pairs={{0,4},{1,5},{2,6},{3,7},{4,8},{5,9},{6,10},{7,11},{8,12},{9,13},{1... | collective-permute-start | bytes 2457608 | tf_op jit(solution)/shard_map/r1/ppermute | solution.py:29
  13.4 5.3 %collective-permute-start.6 = (bf16[400,1024]{1,0:T(8,128)(2,1)S(1)}, bf16[400,1024]{1,0:T(8,128)(2,1)S(1)}, u32[]{:S(2)}, u32[]{:S(2)}) collective-permute-start(bf16[400,1024]{1,0:T(8,128)(2,1)S(1)} %ka.1.args_1_.args_5_), channel_id=1, source_target_pairs={{0,3},{1,0},{2,1},{3,2},{4,7},{5,4},{6,5},{7,6},{8,11},{9,8},{10,9... | collective-permute-start | bytes 2457608 | tf_op jit(solution)/shard_map/ka_down/ppermute | solution.py:29
  19.9 1.0 %s0.1.args_9_ = f32[2,192]{1,0:T(2,128)S(1)} custom-call(bf16[400,1024]{1,0:T(8,128)(2,1)S(1)} %here.1.args_0_, bf16[400,1024]{1,0:T(8,128)(2,1)S(1)} %ka.1.args_1_.args_5_, bf16[400,1024]{1,0:T(8,128)(2,1)S(1)} %kb.1.args_2_.args_6_), custom_call_target="tpu_custom_call" | custom-call | flops 6039797760 | tf_op jit(solution)/shard_map/s0/pallas_call | solution.py:154
  20.9 1.6 %collective-permute-done.1.args_0_.args_3_ = bf16[400,1024]{1,0:T(8,128)(2,1)S(1)} collective-permute-done((bf16[400,1024]{1,0:T(8,128)(2,1)S(1)}, bf16[400,1024]{1,0:T(8,128)(2,1)S(1)}, u32[]{:S(2)}, u32[]{:S(2)}) %collective-permute-start.1) | collective-permute-done | bytes 819232 | tf_op jit(solution)/shard_map/r1/ppermute | solution.py:29
  22.5 2.1 %collective-permute-start.8 = (bf16[400,1024]{1,0:T(8,128)(2,1)S(1)}, bf16[400,1024]{1,0:T(8,128)(2,1)S(1)}, u32[]{:S(2)}, u32[]{:S(2)}) collective-permute-start(bf16[400,1024]{1,0:T(8,128)(2,1)S(1)} %collective-permute-done.1.args_0_.args_3_), channel_id=1, source_target_pairs={{0,32},{1,33},{2,34},{3,35},{4,36},{5,37},{6,38},{7,39},{8,40},{9,... | collective-permute-start | bytes 2457608 | tf_op jit(solution)/shard_map/e1/ppermute | solution.py:29
  24.5 3.0 %collective-permute-start.5 = (bf16[400,1024]{1,0:T(8,128)(2,1)S(1)}, bf16[400,1024]{1,0:T(8,128)(2,1)S(1)}, u32[]{:S(2)}, u32[]{:S(2)}) collective-permute-start(bf16[400,1024]{1,0:T(8,128)(2,1)S(1)} %collective-permute-done.1.args_0_.args_3_), channel_id=1, source_target_pairs={{0,4},{1,5},{2,6},{3,7},{4,8},{5,9},{6,10},{7,11},{8,12},{9,13},{1... | collective-permute-start | bytes 2457608 | tf_op jit(solution)/shard_map/r2/ppermute | solution.py:29
  28.5 2.9 %collective-permute-done.7.args_2_.args_4_ = bf16[400,1024]{1,0:T(8,128)(2,1)S(1)} collective-permute-done((bf16[400,1024]{1,0:T(8,128)(2,1)S(1)}, bf16[400,1024]{1,0:T(8,128)(2,1)S(1)}, u32[]{:S(2)}, u32[]{:S(2)}) %collective-permute-start.7) | collective-permute-done | bytes 819232 | tf_op jit(solution)/shard_map/ka_up/ppermute | solution.py:29
  31.4 1.5 %collective-permute-start.11 = (bf16[400,1024]{1,0:T(8,128)(2,1)S(1)}, bf16[400,1024]{1,0:T(8,128)(2,1)S(1)}, u32[]{:S(2)}, u32[]{:S(2)}) collective-permute-start(bf16[400,1024]{1,0:T(8,128)(2,1)S(1)} %kb.1.args_2_.args_6_), channel_id=1, source_target_pairs={{0,1},{1,2},{2,3},{3,0},{4,5},{5,6},{6,7},{7,4},{8,9},{9,10},{10,1... | collective-permute-start | bytes 2457608 | tf_op jit(solution)/shard_map/kb_up/ppermute | solution.py:29
  32.9 3.0 %s2_.1.args_11_ = f32[6,192]{1,0:T(8,128)S(1)} custom-call(bf16[400,1024]{1,0:T(8,128)(2,1)S(1)} %here.1.args_0_, bf16[400,1024]{1,0:T(8,128)(2,1)S(1)} %collective-permute-done.6.args_1_.args_3_, bf16[400,1024]{1,0:T(8,128)(2,1)S(1)} %collective-permute-done.7.args_2_.args_4_, bf16[400,1024]{1,0:T(8,128)(2,1)S(1)} %collective-permute-done.1.args_0_.args_3_, ...), custom_call_target="tpu_custom_call" | custom-call | flops 24159191040 | tf_op jit(solution)/shard_map/s2/pallas_call | solution.py:154
  36.8 1.8 %collective-permute-start.12 = (bf16[400,1024]{1,0:T(8,128)(2,1)S(1)}, bf16[400,1024]{1,0:T(8,128)(2,1)S(1)}, u32[]{:S(2)}, u32[]{:S(2)}) collective-permute-start(bf16[400,1024]{1,0:T(8,128)(2,1)S(1)} %collective-permute-done.5.args_0_.args_5_), channel_id=1, source_target_pairs={{0,32},{1,33},{2,34},{3,35},{4,36},{5,37},{6,38},{7,39},{8,40},{9,... | collective-permute-start | bytes 2457608 | tf_op jit(solution)/shard_map/e2/ppermute | solution.py:29
  38.6 5.6 %collective-permute-start.9 = (bf16[400,1024]{1,0:T(8,128)(2,1)S(1)}, bf16[400,1024]{1,0:T(8,128)(2,1)S(1)}, u32[]{:S(2)}, u32[]{:S(2)}) collective-permute-start(bf16[400,1024]{1,0:T(8,128)(2,1)S(1)} %collective-permute-done.5.args_0_.args_5_), channel_id=1, source_target_pairs={{0,4},{1,5},{2,6},{3,7},{4,8},{5,9},{6,10},{7,11},{8,12},{9,13},{1... | collective-permute-start | bytes 2457608 | tf_op jit(solution)/shard_map/r3/ppermute | solution.py:29
  44.2 1.6 %s3.1.args_12_ = f32[2,192]{1,0:T(2,128)S(1)} custom-call(bf16[400,1024]{1,0:T(8,128)(2,1)S(1)} %collective-permute-done.5.args_0_.args_5_, bf16[400,1024]{1,0:T(8,128)(2,1)S(1)} %ka.1.args_1_.args_5_, bf16[400,1024]{1,0:T(8,128)(2,1)S(1)} %kb.1.args_2_.args_6_, bf16[400,1024]{1,0:T(8,128)(2,1)S(1)} %collective-permute-done.6.args_1_.args_3_, ...), custom_call_target="tpu_custom_call" | custom-call | flops 12079595520 | tf_op jit(solution)/shard_map/s3/pallas_call | solution.py:154
  45.8 1.6 %s4_.1.args_13_ = f32[2,192]{1,0:T(2,128)S(1)} custom-call(bf16[400,1024]{1,0:T(8,128)(2,1)S(1)} %collective-permute-done.12.args_0_.args_6_, bf16[400,1024]{1,0:T(8,128)(2,1)S(1)} %ka.1.args_1_.args_5_, bf16[400,1024]{1,0:T(8,128)(2,1)S(1)} %kb.1.args_2_.args_6_, bf16[400,1024]{1,0:T(8,128)(2,1)S(1)} %collective-permute-done.6.args_1_.args_3_, ...), custom_call_target="tpu_custom_call" | custom-call | flops 12079595520 | tf_op jit(solution)/shard_map/s4/pallas_call | solution.py:154
  47.4 3.5 %collective-permute-start.15 = (bf16[400,1024]{1,0:T(8,128)(2,1)S(1)}, bf16[400,1024]{1,0:T(8,128)(2,1)S(1)}, u32[]{:S(2)}, u32[]{:S(2)}) collective-permute-start(bf16[400,1024]{1,0:T(8,128)(2,1)S(1)} %collective-permute-done.10.args_1_.args_5_), channel_id=1, source_target_pairs={{0,3},{1,0},{2,1},{3,2},{4,7},{5,4},{6,5},{7,6},{8,11},{9,8},{10,9... | collective-permute-start | bytes 2457608 | tf_op jit(solution)/shard_map/opposite_b/ppermute | solution.py:29
  50.9 3.6 %s5.1.args_14_ = f32[10,192]{1,0:T(8,128)S(1)} custom-call(bf16[400,1024]{1,0:T(8,128)(2,1)S(1)} %here.1.args_0_, bf16[400,1024]{1,0:T(8,128)(2,1)S(1)} %collective-permute-done.10.args_1_.args_5_, bf16[400,1024]{1,0:T(8,128)(2,1)S(1)} %collective-permute-done.11.args_2_.args_6_, bf16[400,1024]{1,0:T(8,128)(2,1)S(1)} %collective-permute-done.1.args_0_.args_3_, ...), custom_call_target="tpu_custom_call" | custom-call | flops 3019898880 | tf_op jit(solution)/shard_map/s5/pallas_call | solution.py:154
  54.9 2.0 %collective-permute-start.13 = (bf16[400,1024]{1,0:T(8,128)(2,1)S(1)}, bf16[400,1024]{1,0:T(8,128)(2,1)S(1)}, u32[]{:S(2)}, u32[]{:S(2)}) collective-permute-start(bf16[400,1024]{1,0:T(8,128)(2,1)S(1)} %collective-permute-done.9.args_0_.args_7_), channel_id=1, source_target_pairs={{0,4},{1,5},{2,6},{3,7},{4,8},{5,9},{6,10},{7,11},{8,12},{9,13},{1... | collective-permute-start | bytes 2457608 | tf_op jit(solution)/shard_map/r4/ppermute | solution.py:29
  56.9 2.3 %s7.1.args_16_ = f32[2,192]{1,0:T(2,128)S(1)} custom-call(bf16[400,1024]{1,0:T(8,128)(2,1)S(1)} %collective-permute-done.9.args_0_.args_7_, bf16[400,1024]{1,0:T(8,128)(2,1)S(1)} %ka.1.args_1_.args_5_, bf16[400,1024]{1,0:T(8,128)(2,1)S(1)} %kb.1.args_2_.args_6_, bf16[400,1024]{1,0:T(8,128)(2,1)S(1)} %collective-permute-done.6.args_1_.args_3_, ...), custom_call_target="tpu_custom_call" | custom-call | flops 18119393280 | tf_op jit(solution)/shard_map/s7/pallas_call | solution.py:154
  59.2 2.3 %s6.1.args_15_ = f32[2,192]{1,0:T(2,128)S(1)} custom-call(bf16[400,1024]{1,0:T(8,128)(2,1)S(1)} %collective-permute-done.16.args_0_.args_8_, bf16[400,1024]{1,0:T(8,128)(2,1)S(1)} %ka.1.args_1_.args_5_, bf16[400,1024]{1,0:T(8,128)(2,1)S(1)} %kb.1.args_2_.args_6_, bf16[400,1024]{1,0:T(8,128)(2,1)S(1)} %collective-permute-done.6.args_1_.args_3_, ...), custom_call_target="tpu_custom_call" | custom-call | flops 1811939328 | tf_op jit(solution)/shard_map/s6/pallas_call | solution.py:154
  61.6 5.0 %s8_.1.args_17_ = f32[14,192]{1,0:T(8,128)S(1)} custom-call(bf16[400,1024]{1,0:T(8,128)(2,1)S(1)} %here.1.args_0_, bf16[400,1024]{1,0:T(8,128)(2,1)S(1)} %collective-permute-done.14.args_1_.args_7_, bf16[400,1024]{1,0:T(8,128)(2,1)S(1)} %collective-permute-done.15.args_2_.args_8_, bf16[400,1024]{1,0:T(8,128)(2,1)S(1)} %collective-permute-done.1.args_0_.args_3_, ...), custom_call_target="tpu_custom_call" | custom-call | flops 4227858432 | tf_op jit(solution)/shard_map/s8/pallas_call | solution.py:154
  66.6 3.0 %s9.1 = f32[16,192]{1,0:T(8,128)S(1)} custom-call(bf16[400,1024]{1,0:T(8,128)(2,1)S(1)} %collective-permute-done.13.args_0_, bf16[400,1024]{1,0:T(8,128)(2,1)S(1)} %ka.1.args_1_.args_5_, bf16[400,1024]{1,0:T(8,128)(2,1)S(1)} %kb.1.args_2_.args_6_, bf16[400,1024]{1,0:T(8,128)(2,1)S(1)} %collective-permute-done.6.args_1_.args_3_, ...), custom_call_target="tpu_custom_call" | custom-call | flops 2415919104 | tf_op jit(solution)/shard_map/s9/pallas_call | solution.py:154
  69.6 14.5 %all_to_all.9 = f32[16,1,192]{2,1,0:T(1,128)S(1)} all-to-all(f32[16,1,192]{2,1,0:T(1,128)S(1)} %copy.4), channel_id=1, replica_groups=mesh['x'=4,'core'=2,'z'=8,'y'=4] {'core','z'}, dimensions={0} | all-to-all | bytes 24576 | tf_op jit(solution)/shard_map/all_to_all | solution.py:240
  (33 shorter events, 6.4 us)
Async XLA Ops:
  0.0 0.7 copy-start.2
  0.0 0.7 copy-start.1
  0.7 1.1 %copy-start = (f32[192,1024]{1,0:T(8,128)S(1)}, f32[192,1024]{1,0:T(8,128)}, u32[]{:S(2)}) copy-start(f32[192,1024]{1,0:T(8,128)} %sketches.1) | copy-start | bytes 2359300
  2.0 5.4 %collective-permute-start = (bf16[208,1024]{1,0:T(8,128)(2,1)S(1)}, bf16[208,1024]{1,0:T(8,128)(2,1)S(1)}, u32[]{:S(2)}, u32[]{:S(2)}) collective-permute-start(bf16[208,1024]{1,0:T(8,128)(2,1)S(1)} %normalise.1.refs_0_), channel_id=1, source_target_pairs={{0,32},{1,33},{2,34},{3,35},{4,36},{5,37},{6,38},{7,39},{8,40},{9,... | collective-permute-start | bytes 1277960 | tf_op jit(solution)/shard_map/partner/ppermute | solution.py:29
  5.3 7.9 %collective-permute-start.2 = (bf16[208,1024]{1,0:T(8,128)(2,1)S(1)}, bf16[208,1024]{1,0:T(8,128)(2,1)S(1)}, u32[]{:S(2)}, u32[]{:S(2)}) collective-permute-start(bf16[208,1024]{1,0:T(8,128)(2,1)S(1)} %normalise.1.refs_0_), channel_id=1, source_target_pairs={{0,192},{1,193},{2,194},{3,195},{4,196},{5,197},{6,198},{7,199},{8... | collective-permute-start | bytes 1277960 | tf_op jit(solution)/shard_map/key_down/ppermute | solution.py:29
  6.3 12.4 %collective-permute-start.3 = (bf16[208,1024]{1,0:T(8,128)(2,1)S(1)}, bf16[208,1024]{1,0:T(8,128)(2,1)S(1)}, u32[]{:S(2)}, u32[]{:S(2)}) collective-permute-start(bf16[208,1024]{1,0:T(8,128)(2,1)S(1)} %normalise.1.refs_0_), channel_id=1, source_target_pairs={{0,128},{1,129},{2,130},{3,131},{4,132},{5,133},{6,134},{7,135},{8... | collective-permute-start | bytes 1277960 | tf_op jit(solution)/shard_map/key_far/ppermute | solution.py:29
  6.7 13.0 %collective-permute-start.4 = (bf16[208,1024]{1,0:T(8,128)(2,1)S(1)}, bf16[208,1024]{1,0:T(8,128)(2,1)S(1)}, u32[]{:S(2)}, u32[]{:S(2)}) collective-permute-start(bf16[208,1024]{1,0:T(8,128)(2,1)S(1)} %normalise.1.refs_0_), channel_id=1, source_target_pairs={{0,64},{1,65},{2,66},{3,67},{4,68},{5,69},{6,70},{7,71},{8,72},{9,... | collective-permute-start | bytes 1277960 | tf_op jit(solution)/shard_map/key_up/ppermute | solution.py:29
  7.6 14.9 %collective-permute-start.1 = (bf16[400,1024]{1,0:T(8,128)(2,1)S(1)}, bf16[400,1024]{1,0:T(8,128)(2,1)S(1)}, u32[]{:S(2)}, u32[]{:S(2)}) collective-permute-start(bf16[400,1024]{1,0:T(8,128)(2,1)S(1)} %here.1.args_0_), channel_id=1, source_target_pairs={{0,4},{1,5},{2,6},{3,7},{4,8},{5,9},{6,10},{7,11},{8,12},{9,13},{1... | collective-permute-start | bytes 2457608 | tf_op jit(solution)/shard_map/r1/ppermute | solution.py:29
  13.4 15.1 %collective-permute-start.6 = (bf16[400,1024]{1,0:T(8,128)(2,1)S(1)}, bf16[400,1024]{1,0:T(8,128)(2,1)S(1)}, u32[]{:S(2)}, u32[]{:S(2)}) collective-permute-start(bf16[400,1024]{1,0:T(8,128)(2,1)S(1)} %ka.1.args_1_.args_5_), channel_id=1, source_target_pairs={{0,3},{1,0},{2,1},{3,2},{4,7},{5,4},{6,5},{7,6},{8,11},{9,8},{10,9... | collective-permute-start | bytes 2457608 | tf_op jit(solution)/shard_map/ka_down/ppermute | solution.py:29
  18.7 12.7 %collective-permute-start.7 = (bf16[400,1024]{1,0:T(8,128)(2,1)S(1)}, bf16[400,1024]{1,0:T(8,128)(2,1)S(1)}, u32[]{:S(2)}, u32[]{:S(2)}) collective-permute-start(bf16[400,1024]{1,0:T(8,128)(2,1)S(1)} %ka.1.args_1_.args_5_), channel_id=1, source_target_pairs={{0,1},{1,2},{2,3},{3,0},{4,5},{5,6},{6,7},{7,4},{8,9},{9,10},{10,1... | collective-permute-start | bytes 2457608 | tf_op jit(solution)/shard_map/ka_up/ppermute | solution.py:29
  22.5 8.9 %collective-permute-start.8 = (bf16[400,1024]{1,0:T(8,128)(2,1)S(1)}, bf16[400,1024]{1,0:T(8,128)(2,1)S(1)}, u32[]{:S(2)}, u32[]{:S(2)}) collective-permute-start(bf16[400,1024]{1,0:T(8,128)(2,1)S(1)} %collective-permute-done.1.args_0_.args_3_), channel_id=1, source_target_pairs={{0,32},{1,33},{2,34},{3,35},{4,36},{5,37},{6,38},{7,39},{8,40},{9,... | collective-permute-start | bytes 2457608 | tf_op jit(solution)/shard_map/e1/ppermute | solution.py:29
  24.5 12.2 %collective-permute-start.5 = (bf16[400,1024]{1,0:T(8,128)(2,1)S(1)}, bf16[400,1024]{1,0:T(8,128)(2,1)S(1)}, u32[]{:S(2)}, u32[]{:S(2)}) collective-permute-start(bf16[400,1024]{1,0:T(8,128)(2,1)S(1)} %collective-permute-done.1.args_0_.args_3_), channel_id=1, source_target_pairs={{0,4},{1,5},{2,6},{3,7},{4,8},{5,9},{6,10},{7,11},{8,12},{9,13},{1... | collective-permute-start | bytes 2457608 | tf_op jit(solution)/shard_map/r2/ppermute | solution.py:29
  31.4 16.0 %collective-permute-start.10 = (bf16[400,1024]{1,0:T(8,128)(2,1)S(1)}, bf16[400,1024]{1,0:T(8,128)(2,1)S(1)}, u32[]{:S(2)}, u32[]{:S(2)}) collective-permute-start(bf16[400,1024]{1,0:T(8,128)(2,1)S(1)} %kb.1.args_2_.args_6_), channel_id=1, source_target_pairs={{0,3},{1,0},{2,1},{3,2},{4,7},{5,4},{6,5},{7,6},{8,11},{9,8},{10,9... | collective-permute-start | bytes 2457608 | tf_op jit(solution)/shard_map/kb_down/ppermute | solution.py:29
  31.4 16.0 %collective-permute-start.11 = (bf16[400,1024]{1,0:T(8,128)(2,1)S(1)}, bf16[400,1024]{1,0:T(8,128)(2,1)S(1)}, u32[]{:S(2)}, u32[]{:S(2)}) collective-permute-start(bf16[400,1024]{1,0:T(8,128)(2,1)S(1)} %kb.1.args_2_.args_6_), channel_id=1, source_target_pairs={{0,1},{1,2},{2,3},{3,0},{4,5},{5,6},{6,7},{7,4},{8,9},{9,10},{10,1... | collective-permute-start | bytes 2457608 | tf_op jit(solution)/shard_map/kb_up/ppermute | solution.py:29
  36.8 9.0 %collective-permute-start.12 = (bf16[400,1024]{1,0:T(8,128)(2,1)S(1)}, bf16[400,1024]{1,0:T(8,128)(2,1)S(1)}, u32[]{:S(2)}, u32[]{:S(2)}) collective-permute-start(bf16[400,1024]{1,0:T(8,128)(2,1)S(1)} %collective-permute-done.5.args_0_.args_5_), channel_id=1, source_target_pairs={{0,32},{1,33},{2,34},{3,35},{4,36},{5,37},{6,38},{7,39},{8,40},{9,... | collective-permute-start | bytes 2457608 | tf_op jit(solution)/shard_map/e2/ppermute | solution.py:29
  38.6 15.9 %collective-permute-start.9 = (bf16[400,1024]{1,0:T(8,128)(2,1)S(1)}, bf16[400,1024]{1,0:T(8,128)(2,1)S(1)}, u32[]{:S(2)}, u32[]{:S(2)}) collective-permute-start(bf16[400,1024]{1,0:T(8,128)(2,1)S(1)} %collective-permute-done.5.args_0_.args_5_), channel_id=1, source_target_pairs={{0,4},{1,5},{2,6},{3,7},{4,8},{5,9},{6,10},{7,11},{8,12},{9,13},{1... | collective-permute-start | bytes 2457608 | tf_op jit(solution)/shard_map/r3/ppermute | solution.py:29
  44.2 17.4 %collective-permute-start.14 = (bf16[400,1024]{1,0:T(8,128)(2,1)S(1)}, bf16[400,1024]{1,0:T(8,128)(2,1)S(1)}, u32[]{:S(2)}, u32[]{:S(2)}) collective-permute-start(bf16[400,1024]{1,0:T(8,128)(2,1)S(1)} %collective-permute-done.7.args_2_.args_4_), channel_id=1, source_target_pairs={{0,1},{1,2},{2,3},{3,0},{4,5},{5,6},{6,7},{7,4},{8,9},{9,10},{10,1... | collective-permute-start | bytes 2457608 | tf_op jit(solution)/shard_map/opposite_a/ppermute | solution.py:29
  47.4 14.1 %collective-permute-start.15 = (bf16[400,1024]{1,0:T(8,128)(2,1)S(1)}, bf16[400,1024]{1,0:T(8,128)(2,1)S(1)}, u32[]{:S(2)}, u32[]{:S(2)}) collective-permute-start(bf16[400,1024]{1,0:T(8,128)(2,1)S(1)} %collective-permute-done.10.args_1_.args_5_), channel_id=1, source_target_pairs={{0,3},{1,0},{2,1},{3,2},{4,7},{5,4},{6,5},{7,6},{8,11},{9,8},{10,9... | collective-permute-start | bytes 2457608 | tf_op jit(solution)/shard_map/opposite_b/ppermute | solution.py:29
  54.5 4.7 %collective-permute-start.16 = (bf16[400,1024]{1,0:T(8,128)(2,1)S(1)}, bf16[400,1024]{1,0:T(8,128)(2,1)S(1)}, u32[]{:S(2)}, u32[]{:S(2)}) collective-permute-start(bf16[400,1024]{1,0:T(8,128)(2,1)S(1)} %collective-permute-done.9.args_0_.args_7_), channel_id=1, source_target_pairs={{0,32},{1,33},{2,34},{3,35},{4,36},{5,37},{6,38},{7,39},{8,40},{9,... | collective-permute-start | bytes 2457608 | tf_op jit(solution)/shard_map/e3/ppermute | solution.py:29
  54.9 11.7 %collective-permute-start.13 = (bf16[400,1024]{1,0:T(8,128)(2,1)S(1)}, bf16[400,1024]{1,0:T(8,128)(2,1)S(1)}, u32[]{:S(2)}, u32[]{:S(2)}) collective-permute-start(bf16[400,1024]{1,0:T(8,128)(2,1)S(1)} %collective-permute-done.9.args_0_.args_7_), channel_id=1, source_target_pairs={{0,4},{1,5},{2,6},{3,7},{4,8},{5,9},{6,10},{7,11},{8,12},{9,13},{1... | collective-permute-start | bytes 2457608 | tf_op jit(solution)/shard_map/r4/ppermute | solution.py:29

commit v5 on v4

--- a/solution.py
+++ b/solution.py
@@ -195,12 +195,13 @@
     after_a, before_a, e1 = after_kernel([after_a, before_a, e1], s1)
     (kb_later,) = after_kernel([kb], before_a)
     after_b, before_b = send(kb_later, second(-1), "kb_down"), send(kb_later, second(1), "kb_up")
-    opposite_a = send(before_a, second(1), "opposite_a")
     near_a = [(after_a, before_a)]
     s2 = score([(here, near_a), (r1, near_a), (e1, base + near_a)], "s2", weight=W2)
     (r2,) = after_kernel([r2], s2)
     r3, e2 = send(r2, along_z, "r3"), send(r2, across, "e2")
     s3 = score([(r2, base + near_a)], "s3", weight=W3)
+    (before_a_later,) = after_kernel([before_a], s3)
+    opposite_a = send(before_a_later, second(1), "opposite_a")
     (e2,) = after_kernel([e2], s3)
     s4 = score([(e2, base + near_a)], "s4", weight=W3)
     after_b, before_b = after_kernel([after_b, before_b], s4)

time: 85 us -> 85 us (level)
  no operation moved by 1% of the time
where the time goes in v5:
time: 85 us; the launch traced here: 84.7 us
  starting transfers between devices  36 us (42%)
  Pallas kernels  25.1 us (30%)
  blocking collectives  14.5 us (17%)
  waiting for transfers between devices  6.43 us (8%)
  local copies, waits for them, and re-layouts  1.84 us (2%)
    ppermute x17, starting transfers between devices, send(): return lax.ppermute(array, AXES, permutation(move))  36 us
    pallas_call x10, Pallas kernels, score(): call(body, jax.ShapeDtypeStruct((total if finish is None else 16, ROWS),...  24.4 us
    all_to_all x1, blocking collectives, on_device(): lax.all_to_all(partial, ('core', 'z'), split_axis=0, concat_axis=0, tiled...  14.5 us
    ppermute x17, waiting for transfers between devices, send(): return lax.ppermute(array, AXES, permutation(move))  6.43 us
    unnamed x6, local copies, waits for them, and re-layouts  1.83 us
  transfers between devices with their start and end apart: 17, of which 4 were waited for; matrix products, arithmetic and copies ran while one was open for 0% of the time, Pallas kernels for 26%

profile of v5, /device:TPU:1, one launch (start us, length us, event | category | flops | bytes accessed | tf_op | source)
XLA Modules:
  0.0 84.7 jit_solution(5897530351658175141)
XLA Ops:
  0.7 1.1 %copy-done = f32[192,1024]{1,0:T(8,128)S(1)} copy-done((f32[192,1024]{1,0:T(8,128)S(1)}, f32[192,1024]{1,0:T(8,128)}, u32[]{:S(2)}) %copy-start) | copy-done | bytes 786456
  2.0 3.3 %collective-permute-start = (bf16[208,1024]{1,0:T(8,128)(2,1)S(1)}, bf16[208,1024]{1,0:T(8,128)(2,1)S(1)}, u32[]{:S(2)}, u32[]{:S(2)}) collective-permute-start(bf16[208,1024]{1,0:T(8,128)(2,1)S(1)} %normalise.1.refs_0_), channel_id=1, source_target_pairs={{0,32},{1,33},{2,34},{3,35},{4,36},{5,37},{6,38},{7,39},{8,40},{9,... | collective-permute-start | bytes 1277960 | tf_op jit(solution)/shard_map/partner/ppermute | solution.py:29
  5.3 1.0 %collective-permute-start.2 = (bf16[208,1024]{1,0:T(8,128)(2,1)S(1)}, bf16[208,1024]{1,0:T(8,128)(2,1)S(1)}, u32[]{:S(2)}, u32[]{:S(2)}) collective-permute-start(bf16[208,1024]{1,0:T(8,128)(2,1)S(1)} %normalise.1.refs_0_), channel_id=1, source_target_pairs={{0,192},{1,193},{2,194},{3,195},{4,196},{5,197},{6,198},{7,199},{8... | collective-permute-start | bytes 1277960 | tf_op jit(solution)/shard_map/key_down/ppermute | solution.py:29
  7.6 5.6 %collective-permute-start.1 = (bf16[400,1024]{1,0:T(8,128)(2,1)S(1)}, bf16[400,1024]{1,0:T(8,128)(2,1)S(1)}, u32[]{:S(2)}, u32[]{:S(2)}) collective-permute-start(bf16[400,1024]{1,0:T(8,128)(2,1)S(1)} %here.1.args_0_), channel_id=1, source_target_pairs={{0,4},{1,5},{2,6},{3,7},{4,8},{5,9},{6,10},{7,11},{8,12},{9,13},{1... | collective-permute-start | bytes 2457608 | tf_op jit(solution)/shard_map/r1/ppermute | solution.py:29
  13.4 5.3 %collective-permute-start.6 = (bf16[400,1024]{1,0:T(8,128)(2,1)S(1)}, bf16[400,1024]{1,0:T(8,128)(2,1)S(1)}, u32[]{:S(2)}, u32[]{:S(2)}) collective-permute-start(bf16[400,1024]{1,0:T(8,128)(2,1)S(1)} %ka.1.args_1_.args_5_), channel_id=1, source_target_pairs={{0,3},{1,0},{2,1},{3,2},{4,7},{5,4},{6,5},{7,6},{8,11},{9,8},{10,9... | collective-permute-start | bytes 2457608 | tf_op jit(solution)/shard_map/ka_down/ppermute | solution.py:29
  19.9 1.0 %s0.1.args_9_ = f32[2,192]{1,0:T(2,128)S(1)} custom-call(bf16[400,1024]{1,0:T(8,128)(2,1)S(1)} %here.1.args_0_, bf16[400,1024]{1,0:T(8,128)(2,1)S(1)} %ka.1.args_1_.args_5_, bf16[400,1024]{1,0:T(8,128)(2,1)S(1)} %kb.1.args_2_.args_6_), custom_call_target="tpu_custom_call" | custom-call | flops 6039797760 | tf_op jit(solution)/shard_map/s0/pallas_call | solution.py:154
  20.9 1.6 %collective-permute-done.1.args_0_.args_3_ = bf16[400,1024]{1,0:T(8,128)(2,1)S(1)} collective-permute-done((bf16[400,1024]{1,0:T(8,128)(2,1)S(1)}, bf16[400,1024]{1,0:T(8,128)(2,1)S(1)}, u32[]{:S(2)}, u32[]{:S(2)}) %collective-permute-start.1) | collective-permute-done | bytes 819232 | tf_op jit(solution)/shard_map/r1/ppermute | solution.py:29
  22.5 2.1 %collective-permute-start.8 = (bf16[400,1024]{1,0:T(8,128)(2,1)S(1)}, bf16[400,1024]{1,0:T(8,128)(2,1)S(1)}, u32[]{:S(2)}, u32[]{:S(2)}) collective-permute-start(bf16[400,1024]{1,0:T(8,128)(2,1)S(1)} %collective-permute-done.1.args_0_.args_3_), channel_id=1, source_target_pairs={{0,32},{1,33},{2,34},{3,35},{4,36},{5,37},{6,38},{7,39},{8,40},{9,... | collective-permute-start | bytes 2457608 | tf_op jit(solution)/shard_map/e1/ppermute | solution.py:29
  24.5 3.0 %collective-permute-start.5 = (bf16[400,1024]{1,0:T(8,128)(2,1)S(1)}, bf16[400,1024]{1,0:T(8,128)(2,1)S(1)}, u32[]{:S(2)}, u32[]{:S(2)}) collective-permute-start(bf16[400,1024]{1,0:T(8,128)(2,1)S(1)} %collective-permute-done.1.args_0_.args_3_), channel_id=1, source_target_pairs={{0,4},{1,5},{2,6},{3,7},{4,8},{5,9},{6,10},{7,11},{8,12},{9,13},{1... | collective-permute-start | bytes 2457608 | tf_op jit(solution)/shard_map/r2/ppermute | solution.py:29
  28.5 2.9 %collective-permute-done.7.args_2_.args_4_ = bf16[400,1024]{1,0:T(8,128)(2,1)S(1)} collective-permute-done((bf16[400,1024]{1,0:T(8,128)(2,1)S(1)}, bf16[400,1024]{1,0:T(8,128)(2,1)S(1)}, u32[]{:S(2)}, u32[]{:S(2)}) %collective-permute-start.7) | collective-permute-done | bytes 819232 | tf_op jit(solution)/shard_map/ka_up/ppermute | solution.py:29
  31.4 1.5 %collective-permute-start.11 = (bf16[400,1024]{1,0:T(8,128)(2,1)S(1)}, bf16[400,1024]{1,0:T(8,128)(2,1)S(1)}, u32[]{:S(2)}, u32[]{:S(2)}) collective-permute-start(bf16[400,1024]{1,0:T(8,128)(2,1)S(1)} %kb.1.args_2_.args_6_), channel_id=1, source_target_pairs={{0,1},{1,2},{2,3},{3,0},{4,5},{5,6},{6,7},{7,4},{8,9},{9,10},{10,1... | collective-permute-start | bytes 2457608 | tf_op jit(solution)/shard_map/kb_up/ppermute | solution.py:29
  32.9 3.0 %s2_.1.args_11_ = f32[6,192]{1,0:T(8,128)S(1)} custom-call(bf16[400,1024]{1,0:T(8,128)(2,1)S(1)} %here.1.args_0_, bf16[400,1024]{1,0:T(8,128)(2,1)S(1)} %collective-permute-done.6.args_1_.args_3_, bf16[400,1024]{1,0:T(8,128)(2,1)S(1)} %collective-permute-done.7.args_2_.args_4_, bf16[400,1024]{1,0:T(8,128)(2,1)S(1)} %collective-permute-done.1.args_0_.args_3_, ...), custom_call_target="tpu_custom_call" | custom-call | flops 24159191040 | tf_op jit(solution)/shard_map/s2/pallas_call | solution.py:154
  36.8 1.8 %collective-permute-start.12 = (bf16[400,1024]{1,0:T(8,128)(2,1)S(1)}, bf16[400,1024]{1,0:T(8,128)(2,1)S(1)}, u32[]{:S(2)}, u32[]{:S(2)}) collective-permute-start(bf16[400,1024]{1,0:T(8,128)(2,1)S(1)} %collective-permute-done.5.args_0_.args_5_), channel_id=1, source_target_pairs={{0,32},{1,33},{2,34},{3,35},{4,36},{5,37},{6,38},{7,39},{8,40},{9,... | collective-permute-start | bytes 2457608 | tf_op jit(solution)/shard_map/e2/ppermute | solution.py:29
  38.6 5.6 %collective-permute-start.9 = (bf16[400,1024]{1,0:T(8,128)(2,1)S(1)}, bf16[400,1024]{1,0:T(8,128)(2,1)S(1)}, u32[]{:S(2)}, u32[]{:S(2)}) collective-permute-start(bf16[400,1024]{1,0:T(8,128)(2,1)S(1)} %collective-permute-done.5.args_0_.args_5_), channel_id=1, source_target_pairs={{0,4},{1,5},{2,6},{3,7},{4,8},{5,9},{6,10},{7,11},{8,12},{9,13},{1... | collective-permute-start | bytes 2457608 | tf_op jit(solution)/shard_map/r3/ppermute | solution.py:29
  44.2 1.6 %s3.1.args_12_ = f32[2,192]{1,0:T(2,128)S(1)} custom-call(bf16[400,1024]{1,0:T(8,128)(2,1)S(1)} %collective-permute-done.5.args_0_.args_5_, bf16[400,1024]{1,0:T(8,128)(2,1)S(1)} %ka.1.args_1_.args_5_, bf16[400,1024]{1,0:T(8,128)(2,1)S(1)} %kb.1.args_2_.args_6_, bf16[400,1024]{1,0:T(8,128)(2,1)S(1)} %collective-permute-done.6.args_1_.args_3_, ...), custom_call_target="tpu_custom_call" | custom-call | flops 12079595520 | tf_op jit(solution)/shard_map/s3/pallas_call | solution.py:154
  45.9 1.6 %s4_.1.args_13_ = f32[2,192]{1,0:T(2,128)S(1)} custom-call(bf16[400,1024]{1,0:T(8,128)(2,1)S(1)} %collective-permute-done.12.args_0_.args_6_, bf16[400,1024]{1,0:T(8,128)(2,1)S(1)} %ka.1.args_1_.args_5_, bf16[400,1024]{1,0:T(8,128)(2,1)S(1)} %kb.1.args_2_.args_6_, bf16[400,1024]{1,0:T(8,128)(2,1)S(1)} %collective-permute-done.6.args_1_.args_3_, ...), custom_call_target="tpu_custom_call" | custom-call | flops 12079595520 | tf_op jit(solution)/shard_map/s4/pallas_call | solution.py:154
  47.5 3.5 %collective-permute-start.15 = (bf16[400,1024]{1,0:T(8,128)(2,1)S(1)}, bf16[400,1024]{1,0:T(8,128)(2,1)S(1)}, u32[]{:S(2)}, u32[]{:S(2)}) collective-permute-start(bf16[400,1024]{1,0:T(8,128)(2,1)S(1)} %collective-permute-done.10.args_1_.args_5_), channel_id=1, source_target_pairs={{0,3},{1,0},{2,1},{3,2},{4,7},{5,4},{6,5},{7,6},{8,11},{9,8},{10,9... | collective-permute-start | bytes 2457608 | tf_op jit(solution)/shard_map/opposite_b/ppermute | solution.py:29
  51.0 3.6 %s5.1.args_14_ = f32[10,192]{1,0:T(8,128)S(1)} custom-call(bf16[400,1024]{1,0:T(8,128)(2,1)S(1)} %here.1.args_0_, bf16[400,1024]{1,0:T(8,128)(2,1)S(1)} %collective-permute-done.10.args_1_.args_5_, bf16[400,1024]{1,0:T(8,128)(2,1)S(1)} %collective-permute-done.11.args_2_.args_6_, bf16[400,1024]{1,0:T(8,128)(2,1)S(1)} %collective-permute-done.1.args_0_.args_3_, ...), custom_call_target="tpu_custom_call" | custom-call | flops 3019898880 | tf_op jit(solution)/shard_map/s5/pallas_call | solution.py:154
  54.9 2.0 %collective-permute-start.13 = (bf16[400,1024]{1,0:T(8,128)(2,1)S(1)}, bf16[400,1024]{1,0:T(8,128)(2,1)S(1)}, u32[]{:S(2)}, u32[]{:S(2)}) collective-permute-start(bf16[400,1024]{1,0:T(8,128)(2,1)S(1)} %collective-permute-done.9.args_0_.args_7_), channel_id=1, source_target_pairs={{0,4},{1,5},{2,6},{3,7},{4,8},{5,9},{6,10},{7,11},{8,12},{9,13},{1... | collective-permute-start | bytes 2457608 | tf_op jit(solution)/shard_map/r4/ppermute | solution.py:29
  56.9 2.3 %s7.1.args_16_ = f32[2,192]{1,0:T(2,128)S(1)} custom-call(bf16[400,1024]{1,0:T(8,128)(2,1)S(1)} %collective-permute-done.9.args_0_.args_7_, bf16[400,1024]{1,0:T(8,128)(2,1)S(1)} %ka.1.args_1_.args_5_, bf16[400,1024]{1,0:T(8,128)(2,1)S(1)} %kb.1.args_2_.args_6_, bf16[400,1024]{1,0:T(8,128)(2,1)S(1)} %collective-permute-done.6.args_1_.args_3_, ...), custom_call_target="tpu_custom_call" | custom-call | flops 18119393280 | tf_op jit(solution)/shard_map/s7/pallas_call | solution.py:154
  59.2 2.3 %s6.1.args_15_ = f32[2,192]{1,0:T(2,128)S(1)} custom-call(bf16[400,1024]{1,0:T(8,128)(2,1)S(1)} %collective-permute-done.16.args_0_.args_8_, bf16[400,1024]{1,0:T(8,128)(2,1)S(1)} %ka.1.args_1_.args_5_, bf16[400,1024]{1,0:T(8,128)(2,1)S(1)} %kb.1.args_2_.args_6_, bf16[400,1024]{1,0:T(8,128)(2,1)S(1)} %collective-permute-done.6.args_1_.args_3_, ...), custom_call_target="tpu_custom_call" | custom-call | flops 1811939328 | tf_op jit(solution)/shard_map/s6/pallas_call | solution.py:154
  61.6 5.0 %s8_.1.args_17_ = f32[14,192]{1,0:T(8,128)S(1)} custom-call(bf16[400,1024]{1,0:T(8,128)(2,1)S(1)} %here.1.args_0_, bf16[400,1024]{1,0:T(8,128)(2,1)S(1)} %collective-permute-done.14.args_1_.args_7_, bf16[400,1024]{1,0:T(8,128)(2,1)S(1)} %collective-permute-done.15.args_2_.args_8_, bf16[400,1024]{1,0:T(8,128)(2,1)S(1)} %collective-permute-done.1.args_0_.args_3_, ...), custom_call_target="tpu_custom_call" | custom-call | flops 4227858432 | tf_op jit(solution)/shard_map/s8/pallas_call | solution.py:154
  66.6 3.0 %s9.1 = f32[16,192]{1,0:T(8,128)S(1)} custom-call(bf16[400,1024]{1,0:T(8,128)(2,1)S(1)} %collective-permute-done.13.args_0_, bf16[400,1024]{1,0:T(8,128)(2,1)S(1)} %ka.1.args_1_.args_5_, bf16[400,1024]{1,0:T(8,128)(2,1)S(1)} %kb.1.args_2_.args_6_, bf16[400,1024]{1,0:T(8,128)(2,1)S(1)} %collective-permute-done.6.args_1_.args_3_, ...), custom_call_target="tpu_custom_call" | custom-call | flops 2415919104 | tf_op jit(solution)/shard_map/s9/pallas_call | solution.py:154
  69.6 14.5 %all_to_all.9 = f32[16,1,192]{2,1,0:T(1,128)S(1)} all-to-all(f32[16,1,192]{2,1,0:T(1,128)S(1)} %copy.4), channel_id=1, replica_groups=mesh['x'=4,'core'=2,'z'=8,'y'=4] {'core','z'}, dimensions={0} | all-to-all | bytes 24576 | tf_op jit(solution)/shard_map/all_to_all | solution.py:241
  (33 shorter events, 6.4 us)
Async XLA Ops:
  0.0 0.7 copy-start.2
  0.0 0.7 copy-start.1
  0.7 1.1 %copy-start = (f32[192,1024]{1,0:T(8,128)S(1)}, f32[192,1024]{1,0:T(8,128)}, u32[]{:S(2)}) copy-start(f32[192,1024]{1,0:T(8,128)} %sketches.1) | copy-start | bytes 2359300
  2.0 5.4 %collective-permute-start = (bf16[208,1024]{1,0:T(8,128)(2,1)S(1)}, bf16[208,1024]{1,0:T(8,128)(2,1)S(1)}, u32[]{:S(2)}, u32[]{:S(2)}) collective-permute-start(bf16[208,1024]{1,0:T(8,128)(2,1)S(1)} %normalise.1.refs_0_), channel_id=1, source_target_pairs={{0,32},{1,33},{2,34},{3,35},{4,36},{5,37},{6,38},{7,39},{8,40},{9,... | collective-permute-start | bytes 1277960 | tf_op jit(solution)/shard_map/partner/ppermute | solution.py:29
  5.3 7.9 %collective-permute-start.2 = (bf16[208,1024]{1,0:T(8,128)(2,1)S(1)}, bf16[208,1024]{1,0:T(8,128)(2,1)S(1)}, u32[]{:S(2)}, u32[]{:S(2)}) collective-permute-start(bf16[208,1024]{1,0:T(8,128)(2,1)S(1)} %normalise.1.refs_0_), channel_id=1, source_target_pairs={{0,192},{1,193},{2,194},{3,195},{4,196},{5,197},{6,198},{7,199},{8... | collective-permute-start | bytes 1277960 | tf_op jit(solution)/shard_map/key_down/ppermute | solution.py:29
  6.3 12.4 %collective-permute-start.3 = (bf16[208,1024]{1,0:T(8,128)(2,1)S(1)}, bf16[208,1024]{1,0:T(8,128)(2,1)S(1)}, u32[]{:S(2)}, u32[]{:S(2)}) collective-permute-start(bf16[208,1024]{1,0:T(8,128)(2,1)S(1)} %normalise.1.refs_0_), channel_id=1, source_target_pairs={{0,128},{1,129},{2,130},{3,131},{4,132},{5,133},{6,134},{7,135},{8... | collective-permute-start | bytes 1277960 | tf_op jit(solution)/shard_map/key_far/ppermute | solution.py:29
  6.7 13.0 %collective-permute-start.4 = (bf16[208,1024]{1,0:T(8,128)(2,1)S(1)}, bf16[208,1024]{1,0:T(8,128)(2,1)S(1)}, u32[]{:S(2)}, u32[]{:S(2)}) collective-permute-start(bf16[208,1024]{1,0:T(8,128)(2,1)S(1)} %normalise.1.refs_0_), channel_id=1, source_target_pairs={{0,64},{1,65},{2,66},{3,67},{4,68},{5,69},{6,70},{7,71},{8,72},{9,... | collective-permute-start | bytes 1277960 | tf_op jit(solution)/shard_map/key_up/ppermute | solution.py:29
  7.6 14.9 %collective-permute-start.1 = (bf16[400,1024]{1,0:T(8,128)(2,1)S(1)}, bf16[400,1024]{1,0:T(8,128)(2,1)S(1)}, u32[]{:S(2)}, u32[]{:S(2)}) collective-permute-start(bf16[400,1024]{1,0:T(8,128)(2,1)S(1)} %here.1.args_0_), channel_id=1, source_target_pairs={{0,4},{1,5},{2,6},{3,7},{4,8},{5,9},{6,10},{7,11},{8,12},{9,13},{1... | collective-permute-start | bytes 2457608 | tf_op jit(solution)/shard_map/r1/ppermute | solution.py:29
  13.4 15.1 %collective-permute-start.6 = (bf16[400,1024]{1,0:T(8,128)(2,1)S(1)}, bf16[400,1024]{1,0:T(8,128)(2,1)S(1)}, u32[]{:S(2)}, u32[]{:S(2)}) collective-permute-start(bf16[400,1024]{1,0:T(8,128)(2,1)S(1)} %ka.1.args_1_.args_5_), channel_id=1, source_target_pairs={{0,3},{1,0},{2,1},{3,2},{4,7},{5,4},{6,5},{7,6},{8,11},{9,8},{10,9... | collective-permute-start | bytes 2457608 | tf_op jit(solution)/shard_map/ka_down/ppermute | solution.py:29
  18.7 12.7 %collective-permute-start.7 = (bf16[400,1024]{1,0:T(8,128)(2,1)S(1)}, bf16[400,1024]{1,0:T(8,128)(2,1)S(1)}, u32[]{:S(2)}, u32[]{:S(2)}) collective-permute-start(bf16[400,1024]{1,0:T(8,128)(2,1)S(1)} %ka.1.args_1_.args_5_), channel_id=1, source_target_pairs={{0,1},{1,2},{2,3},{3,0},{4,5},{5,6},{6,7},{7,4},{8,9},{9,10},{10,1... | collective-permute-start | bytes 2457608 | tf_op jit(solution)/shard_map/ka_up/ppermute | solution.py:29
  22.5 8.9 %collective-permute-start.8 = (bf16[400,1024]{1,0:T(8,128)(2,1)S(1)}, bf16[400,1024]{1,0:T(8,128)(2,1)S(1)}, u32[]{:S(2)}, u32[]{:S(2)}) collective-permute-start(bf16[400,1024]{1,0:T(8,128)(2,1)S(1)} %collective-permute-done.1.args_0_.args_3_), channel_id=1, source_target_pairs={{0,32},{1,33},{2,34},{3,35},{4,36},{5,37},{6,38},{7,39},{8,40},{9,... | collective-permute-start | bytes 2457608 | tf_op jit(solution)/shard_map/e1/ppermute | solution.py:29
  24.5 12.2 %collective-permute-start.5 = (bf16[400,1024]{1,0:T(8,128)(2,1)S(1)}, bf16[400,1024]{1,0:T(8,128)(2,1)S(1)}, u32[]{:S(2)}, u32[]{:S(2)}) collective-permute-start(bf16[400,1024]{1,0:T(8,128)(2,1)S(1)} %collective-permute-done.1.args_0_.args_3_), channel_id=1, source_target_pairs={{0,4},{1,5},{2,6},{3,7},{4,8},{5,9},{6,10},{7,11},{8,12},{9,13},{1... | collective-permute-start | bytes 2457608 | tf_op jit(solution)/shard_map/r2/ppermute | solution.py:29
  31.4 16.1 %collective-permute-start.10 = (bf16[400,1024]{1,0:T(8,128)(2,1)S(1)}, bf16[400,1024]{1,0:T(8,128)(2,1)S(1)}, u32[]{:S(2)}, u32[]{:S(2)}) collective-permute-start(bf16[400,1024]{1,0:T(8,128)(2,1)S(1)} %kb.1.args_2_.args_6_), channel_id=1, source_target_pairs={{0,3},{1,0},{2,1},{3,2},{4,7},{5,4},{6,5},{7,6},{8,11},{9,8},{10,9... | collective-permute-start | bytes 2457608 | tf_op jit(solution)/shard_map/kb_down/ppermute | solution.py:29
  31.4 16.1 %collective-permute-start.11 = (bf16[400,1024]{1,0:T(8,128)(2,1)S(1)}, bf16[400,1024]{1,0:T(8,128)(2,1)S(1)}, u32[]{:S(2)}, u32[]{:S(2)}) collective-permute-start(bf16[400,1024]{1,0:T(8,128)(2,1)S(1)} %kb.1.args_2_.args_6_), channel_id=1, source_target_pairs={{0,1},{1,2},{2,3},{3,0},{4,5},{5,6},{6,7},{7,4},{8,9},{9,10},{10,1... | collective-permute-start | bytes 2457608 | tf_op jit(solution)/shard_map/kb_up/ppermute | solution.py:29
  36.8 9.1 %collective-permute-start.12 = (bf16[400,1024]{1,0:T(8,128)(2,1)S(1)}, bf16[400,1024]{1,0:T(8,128)(2,1)S(1)}, u32[]{:S(2)}, u32[]{:S(2)}) collective-permute-start(bf16[400,1024]{1,0:T(8,128)(2,1)S(1)} %collective-permute-done.5.args_0_.args_5_), channel_id=1, source_target_pairs={{0,32},{1,33},{2,34},{3,35},{4,36},{5,37},{6,38},{7,39},{8,40},{9,... | collective-permute-start | bytes 2457608 | tf_op jit(solution)/shard_map/e2/ppermute | solution.py:29
  38.6 16.0 %collective-permute-start.9 = (bf16[400,1024]{1,0:T(8,128)(2,1)S(1)}, bf16[400,1024]{1,0:T(8,128)(2,1)S(1)}, u32[]{:S(2)}, u32[]{:S(2)}) collective-permute-start(bf16[400,1024]{1,0:T(8,128)(2,1)S(1)} %collective-permute-done.5.args_0_.args_5_), channel_id=1, source_target_pairs={{0,4},{1,5},{2,6},{3,7},{4,8},{5,9},{6,10},{7,11},{8,12},{9,13},{1... | collective-permute-start | bytes 2457608 | tf_op jit(solution)/shard_map/r3/ppermute | solution.py:29
  45.8 15.8 %collective-permute-start.14 = (bf16[400,1024]{1,0:T(8,128)(2,1)S(1)}, bf16[400,1024]{1,0:T(8,128)(2,1)S(1)}, u32[]{:S(2)}, u32[]{:S(2)}) collective-permute-start(bf16[400,1024]{1,0:T(8,128)(2,1)S(1)} %collective-permute-done.7.args_2_.args_4_), channel_id=1, source_target_pairs={{0,1},{1,2},{2,3},{3,0},{4,5},{5,6},{6,7},{7,4},{8,9},{9,10},{10,1... | collective-permute-start | bytes 2457608 | tf_op jit(solution)/shard_map/opposite_a/ppermute | solution.py:29
  47.5 14.1 %collective-permute-start.15 = (bf16[400,1024]{1,0:T(8,128)(2,1)S(1)}, bf16[400,1024]{1,0:T(8,128)(2,1)S(1)}, u32[]{:S(2)}, u32[]{:S(2)}) collective-permute-start(bf16[400,1024]{1,0:T(8,128)(2,1)S(1)} %collective-permute-done.10.args_1_.args_5_), channel_id=1, source_target_pairs={{0,3},{1,0},{2,1},{3,2},{4,7},{5,4},{6,5},{7,6},{8,11},{9,8},{10,9... | collective-permute-start | bytes 2457608 | tf_op jit(solution)/shard_map/opposite_b/ppermute | solution.py:29
  54.6 4.6 %collective-permute-start.16 = (bf16[400,1024]{1,0:T(8,128)(2,1)S(1)}, bf16[400,1024]{1,0:T(8,128)(2,1)S(1)}, u32[]{:S(2)}, u32[]{:S(2)}) collective-permute-start(bf16[400,1024]{1,0:T(8,128)(2,1)S(1)} %collective-permute-done.9.args_0_.args_7_), channel_id=1, source_target_pairs={{0,32},{1,33},{2,34},{3,35},{4,36},{5,37},{6,38},{7,39},{8,40},{9,... | collective-permute-start | bytes 2457608 | tf_op jit(solution)/shard_map/e3/ppermute | solution.py:29
  54.9 11.7 %collective-permute-start.13 = (bf16[400,1024]{1,0:T(8,128)(2,1)S(1)}, bf16[400,1024]{1,0:T(8,128)(2,1)S(1)}, u32[]{:S(2)}, u32[]{:S(2)}) collective-permute-start(bf16[400,1024]{1,0:T(8,128)(2,1)S(1)} %collective-permute-done.9.args_0_.args_7_), channel_id=1, source_target_pairs={{0,4},{1,5},{2,6},{3,7},{4,8},{5,9},{6,10},{7,11},{8,12},{9,13},{1... | collective-permute-start | bytes 2457608 | tf_op jit(solution)/shard_map/r4/ppermute | solution.py:29
